TPU v7x, 128 devices: a whole 4x4x4 slice. The times are simulated.
128 devices in a mesh: section: 4 (over y), seq: 8 (over x, core), tp: 4 (over z).
Axes of the slice: x: 4, y: 4, z: 4, core: 2. Of those that a mesh axis runs over, the one named last changes fastest.
Arguments:
- queries: bfloat16 [12288, 4096], P(('section', 'seq'), 'tp'), may hold values from -200 to 200
- neighbours: bfloat16 [49152, 4096], P(('section', 'seq'), 'tp'), may hold values from -400 to 400
- norm_gain: float32 [4096], replicated, may hold values from 0.1 to 1.9
- key_weight: bfloat16 [4, 4096, 4096], P('section', None, 'tp'), may hold values from -0.09375 to 0.09375
- value_weight: bfloat16 [4, 4096, 4096], P('section', None, 'tp'), may hold values from -0.09375 to 0.09375
- slot_anchor: int32 [768], P(('section', 'seq')), may hold values from 0 to 767, as said below
- nbr_count: int32 [192], P(('section', 'seq')), may hold values from 1 to 2, as said below
Outputs:
- attended: bfloat16 [12288, 4096], P(('section', 'seq'), 'tp')
Inputs may be any that keep to these rules, and one draw needn't show every extreme that they name: `slot_anchor`: every piece fills exactly one slot. The slots of one block name pieces of exactly 12 blocks, two pieces from each. `nbr_count`: how many of a stretch's neighbours are usable; some blocks have far more usable neighbours than others.
All inputs are finite; a program needn't handle non-finite values.
Results may differ from a plain program's by a relative error of at most 0.004.
The roundings to bfloat16 on the way count: a program that leaves them out, or rounds other values in their place, can miss the bound.
Values may be sent and summed in bfloat16 or wider, within the bound.
No kernel may reach another device: no remote copies, remote signals or barrier semaphores. Data moves between devices by JAX's collectives and lax.ppermute only.
A program may use at most 128 MiB of HBM per device.

v0:
```python
import jax
import jax.numpy as jnp
from jax import lax
from jax.sharding import PartitionSpec as P

HD = 128
PIECE = 64
NBR = 2


norm_eps = 1e-05


def attend(query_rows, key_rows, value_rows, stretch_counts):
    stretch_total = stretch_counts.shape[0]
    head_count = query_rows.shape[1] // HD
    key_span = key_rows.shape[0] // stretch_total
    query_heads = query_rows.reshape(stretch_total, -1, head_count, HD)
    key_heads = key_rows.reshape(stretch_total, key_span, head_count, HD)
    value_heads = value_rows.reshape(stretch_total, key_span, head_count, HD)
    scores = jnp.einsum(
        "cqhd,ckhd->chqk", query_heads, key_heads, preferred_element_type=jnp.float32
    ) * HD ** (-0.5)
    neighbour_of_key = jnp.arange(key_span, dtype=jnp.int32) // (key_span // NBR)
    usable = neighbour_of_key[None, :] < stretch_counts[:, None]
    scores = jnp.where(usable[:, None, None, :], scores, -1e30)
    row_max = jnp.max(scores, -1, keepdims=True)
    exponents = jnp.exp(scores - row_max)
    weights = (exponents / jnp.sum(exponents, -1, keepdims=True)).astype(jnp.bfloat16)
    combined = jnp.einsum(
        "chqk,ckhd->cqhd", weights, value_heads, preferred_element_type=jnp.float32
    )
    return combined.astype(jnp.bfloat16).reshape(query_rows.shape)


def per_device(queries, neighbours, norm_gain, key_weight, value_weight, slot_anchor, nbr_count):
    owners = lax.axis_size("section") * lax.axis_size("seq")
    slot_count = slot_anchor.shape[0]
    width_part = neighbours.shape[1]
    capacity = 2 * ((slot_count // 2 + owners - 1) // owners)
    key_matrix = key_weight[0]
    value_matrix = value_weight[0]
    source = slot_anchor // slot_count
    unit_index = slot_anchor % slot_count
    earlier = (source[None, :] == source[:, None]) & (slot_anchor[None, :] < slot_anchor[:, None])
    rank_among = jnp.sum(earlier.astype(jnp.int32), 1)
    grid_cell = source * capacity + rank_among
    cell_match = grid_cell[None, :] == jnp.arange(owners * capacity, dtype=jnp.int32)[:, None]
    request = jnp.sum(jnp.where(cell_match, unit_index[None, :] + 1, 0), 1) - 1
    request = request.reshape(owners, capacity)
    asked_units = lax.all_to_all(
        request, ("section", "seq"), split_axis=0, concat_axis=0, tiled=True
    )
    pieces = neighbours.reshape(slot_count, PIECE, width_part)
    picked = jnp.take(pieces, jnp.clip(asked_units, 0, slot_count - 1), axis=0)
    picked = jnp.where((asked_units >= 0)[:, :, None, None], picked, jnp.zeros_like(picked))
    arrived = lax.all_to_all(picked, ("section", "seq"), split_axis=0, concat_axis=0, tiled=True)
    arrived = arrived.reshape(owners * capacity, PIECE, width_part)
    own_pieces = jnp.take(arrived, grid_cell, axis=0).reshape(slot_count * PIECE, width_part)
    full_rows = lax.all_gather(own_pieces, "tp", axis=1, tiled=True)
    row_values = full_rows.astype(jnp.float32)
    mean_square = jnp.mean(row_values * row_values, -1, keepdims=True)
    encoded = (row_values * lax.rsqrt(mean_square + norm_eps) * norm_gain).astype(jnp.bfloat16)
    key_sums = jnp.dot(encoded, key_matrix, preferred_element_type=jnp.float32)
    value_sums = jnp.dot(encoded, value_matrix, preferred_element_type=jnp.float32)
    key_rows = key_sums.astype(jnp.bfloat16)
    value_rows = value_sums.astype(jnp.bfloat16)
    return attend(queries, key_rows, value_rows, nbr_count)


def solution(mesh):
    in_specs = (
        P(("section", "seq"), "tp"),
        P(("section", "seq"), "tp"),
        P(),
        P("section", None, "tp"),
        P("section", None, "tp"),
        P(("section", "seq")),
        P(("section", "seq")),
    )
    out_specs = P(("section", "seq"), "tp")
    return jax.shard_map(
        per_device, mesh=mesh, in_specs=in_specs, out_specs=out_specs, check_vma=False
    )
```

profile of v0, /device:TPU:2, one launch (start us, length us, event | category | flops | bytes accessed | tf_op | source)
XLA Modules:
  0.0 326.9 jit_solution(1473352754198231703)
XLA Ops:
  6.5 0.8 and_select_fusion.2
  7.4 1.0 convert_reduce_fusion
  8.4 0.1 select_reduce_fusion
  8.5 0.1 sub.26
  8.6 13.6 %all_to_all.11 = s32[32,1,2]{2,1,0:T(1,128)S(1)} all-to-all(s32[32,1,2]{2,1,0:T(1,128)S(1)} %bitcast.64), channel_id=1, replica_groups=mesh['section'=4,'seq'=8,'tp'=4] {'section','seq'}, dimensions={0} | all-to-all | bytes 512 | tf_op jit(solution)/shard_map/all_to_all | solution.py:51
  22.1 0.1 copy.50
  22.2 0.1 copy.54
  22.3 0.1 reshape.142
  22.5 0.1 copy.53
  22.6 0.1 copy.51
  22.7 5.4 %gather_fusion = bf16[64,64,1024]{2,1,0:T(8,128)(2,1)} fusion(bf16[24,64,1024]{2,1,0:T(8,128)(2,1)S(1)} %bitcast.57, s32[1024]{0:T(1024)S(1)} %pad_clamp_fusion.1), kind=kCustom, calls=%fused_computation | custom fusion | bytes 16777472 | tf_op jit(solution)/shard_map/jit(_take)/gather | solution.py:55
  28.0 7.6 %select_select_fusion = bf16[32,2,64,1024]{3,2,1,0:T(8,128)(2,1)} fusion(bf16[32,2,64,1024]{3,2,1,0:T(8,128)(2,1)} %bitcast.58, pred[32,2]{1,0:T(8,128)(4,1)S(1)} %copy.53, pred[32,2]{1,0:T(8,128)(4,1)S(1)} %copy.51), kind=kLoop, calls=%fused_computation.12 | loop fusion | flops 8388608 | bytes 16777344 | tf_op jit(solution)/shard_map/jit(_where)/select_n | solution.py:56
  35.7 6.1 %all-to-all-start.1 = ((bf16[32,2,64,1024]{3,2,1,0:T(8,128)(2,1)}), bf16[32,2,64,1024]{3,2,1,0:T(8,128)(2,1)}, u32[]{:S(2)}, u32[]{:S(2)}) async-start(bf16[32,2,64,1024]{3,2,1,0:T(8,128)(2,1)} %select_select_fusion), calls=%async_computation.1 | async-start | bytes 16777216 | tf_op jit(solution)/shard_map/all_to_all | solution.py:57
  41.8 0.1 broadcast_in_dim.76
  41.8 0.1 broadcast_in_dim.77
  41.9 99.5 %all-to-all-done.1 = bf16[32,2,64,1024]{3,2,1,0:T(8,128)(2,1)} async-done(((bf16[32,2,64,1024]{3,2,1,0:T(8,128)(2,1)}), bf16[32,2,64,1024]{3,2,1,0:T(8,128)(2,1)}, u32[]{:S(2)}, u32[]{:S(2)}) %all-to-all-start.1) | async-done | bytes 8388640 | tf_op jit(solution)/shard_map/all_to_all | solution.py:57
  141.4 4.1 %gather_fusion.1 = bf16[24,64,1024]{2,1,0:T(8,128)(2,1)S(1)} fusion(bf16[64,64,1024]{2,1,0:T(8,128)(2,1)} %bitcast.6, s32[1024]{0:T(1024)S(1)} %pad_clamp_fusion), kind=kCustom, calls=%fused_computation.1 | custom fusion | bytes 6291552 | tf_op jit(solution)/shard_map/jit(_take)/gather | solution.py:59
  145.6 2.1 bitcast_select_fusion
  147.8 1.1 copy-done.4
  148.9 1.1 copy.60
  150.0 120.2 %all-gather.2.cloned.1.call-done = bf16[1536,4096]{1,0:T(8,128)(2,1)} async-done(((bf16[1536,1024]{1,0:T(8,128)(2,1)}), bf16[1536,4096]{1,0:T(8,128)(2,1)}) %all-gather.2.cloned.1.call-update) | async-done | bytes 12582928 | tf_op jit(solution)/shard_map/all_gather | solution.py:60
  270.2 7.1 %fusion.1 = f32[1536]{0:T(1024)S(1)} fusion(bf16[1536,4096]{1,0:T(8,128)(2,1)} %all-gather.2.cloned.1.call-done), kind=kLoop, calls=%fused_computation.5 | loop fusion | flops 18872832 | bytes 12589056 | tf_op jit(solution)/shard_map/reduce_sum | solution.py:62
  277.3 18.7 %fusion.29 = bf16[192,8,8,128]{3,1,2,0:T(8,128)(2,1)S(1)} fusion(bf16[1,4096,1024]{2,1,0:T(8,128)(2,1)} %param.11, bf16[1536,4096]{1,0:T(8,128)(2,1)} %all-gather.2.cloned.1.call-done, f32[4096]{0:T(1024)S(1)} %copy-done.6, f32[1536]{0:T(1024)S(1)} %add_rsqrt_fusion), kind=kOutput, calls=%fused_computation.27 | convolution fusion | flops 12911640576 | bytes 24139776 | tf_op jit(solution)/shard_map/dot_general | solution.py:65
  296.0 0.8 copy.61
  296.8 16.7 %fusion.24 = bf16[192,8,8,128]{3,1,2,0:T(8,128)(2,1)S(1)} fusion(bf16[1,4096,1024]{2,1,0:T(8,128)(2,1)} %param.10, bf16[1536,4096]{1,0:T(8,128)(2,1)S(1)} %copy-done.2, f32[4096]{0:T(1024)S(1)} %copy-done.6, f32[1536]{0:T(1024)S(1)} %add_rsqrt_fusion), kind=kOutput, calls=%fused_computation.26 | convolution fusion | flops 12911640576 | bytes 24139776 | tf_op jit(solution)/shard_map/dot_general | solution.py:64
  313.5 0.8 copy.59
  314.4 0.3 copy-done.3
  314.6 1.2 fusion.20
  315.9 1.6 fusion.48
  317.4 1.0 fusion.41
  318.5 0.5 copy.58
  319.0 1.1 copy.74
  (25 shorter events, 0.2 us)
Async XLA Ops:
  6.5 16.1 %copy-start = (bf16[1536,1024]{1,0:T(8,128)(2,1)S(1)}, bf16[1536,1024]{1,0:T(8,128)(2,1)}, u32[]{:S(2)}) copy-start(bf16[1536,1024]{1,0:T(8,128)(2,1)} %param.8) | copy-start | bytes 9437188
  35.7 105.8 %all-to-all-start.1 = ((bf16[32,2,64,1024]{3,2,1,0:T(8,128)(2,1)}), bf16[32,2,64,1024]{3,2,1,0:T(8,128)(2,1)}, u32[]{:S(2)}, u32[]{:S(2)}) async-start(bf16[32,2,64,1024]{3,2,1,0:T(8,128)(2,1)} %select_select_fusion), calls=%async_computation.1 | async-start | bytes 16777216 | tf_op jit(solution)/shard_map/all_to_all | solution.py:57
  41.7 228.5 %all-gather.2.cloned.1.call-start = ((), (), s32[]{:S(2)}) async-start(), calls=%async_computation.2 | async-start | bytes 15728640 | tf_op jit(solution)/shard_map/all_gather | solution.py:60
  147.7 1.1 copy-start.4
  147.7 2.2 copy-start.5
  150.0 127.3 %copy-start.6 = (f32[4096]{0:T(1024)S(1)}, f32[4096]{0:T(1024)}, u32[]{:S(2)}) copy-start(f32[4096]{0:T(1024)} %param.9) | copy-start | bytes 49156
  277.3 19.5 %copy-start.2 = (bf16[1536,4096]{1,0:T(8,128)(2,1)S(1)}, bf16[1536,4096]{1,0:T(8,128)(2,1)}, u32[]{:S(2)}) copy-start(bf16[1536,4096]{1,0:T(8,128)(2,1)} %all-gather.2.cloned.1.call-done) | copy-start | bytes 37748740
  313.5 1.1 copy-start.3
  317.4 2.6 copy-start.1
Sparse Core Ops, SparseCore 0:
  147.9 122.2 all-gather.1
where the time goes:
time: 328 us; the launch traced here: 327 us
  waiting for transfers between devices  220 us (67%)
  matrix products  37.6 us (11%)
  other arithmetic  20.4 us (6%)
  local copies, waits for them, and re-layouts  16 us (5%)
  blocking collectives  13.6 us (4%)
  between operations  13.6 us (4%)
  starting transfers between devices  6.09 us (2%)
    all_gather x1, waiting for transfers between devices, per_device(): full_rows = lax.all_gather(own_pieces, 'tp', axis=1, tiled=True)  120 us
    all_to_all x1, waiting for transfers between devices, per_device(): lax.all_to_all(picked, ('section', 'seq'), split_axis=0, concat_axis=0, t...  99.5 us
    dot_general x1, matrix products, per_device(): jnp.dot(encoded, value_matrix, preferred_element_type=jnp.float32)  18.7 us
    dot_general x1, matrix products, per_device(): key_sums = jnp.dot(encoded, key_matrix, preferred_element_type=jnp.float32)  16.7 us
    all_to_all x1, blocking collectives, per_device(): lax.all_to_all(request, ('section', 'seq'), split_axis=0, concat_axis=0,...  13.6 us
    select_n x1, other arithmetic, per_device(): jnp.where((asked_units >= 0)[:, :, None, None], picked, jnp.zeros_like(pi...  7.62 us
    reduce_sum x1, other arithmetic, per_device(): mean_square = jnp.mean(row_values * row_values, -1, keepdims=True)  7.07 us
  transfers between devices with their start and end apart: 2, of which 2 were waited for; matrix products, arithmetic and copies ran while one was open for 0% of the time, Pallas kernels for 0%

commit v1 on v0

v1 whole, which is shorter than its diff:
```python
import functools

import jax
import jax.numpy as jnp
from jax import lax
from jax.experimental import pallas as pl
from jax.experimental.pallas import tpu as pltpu
from jax.sharding import PartitionSpec as P

HD = 128
PIECE = 64
NBR = 2
CHUNKS = (16, 16, 16, 16)
MODE = ("offload", "ring", "offload", "ring")
EPS = 1e-05
OWN = ("section", "seq")
KERNEL_VMEM = 62 << 20


def scatter_rows(position, pieces, offset, rows, cells):
    count, _, width = pieces.shape

    def body(position_ref, pieces_ref, out_ref, held, sem, sems):
        load = pltpu.make_async_copy(pieces_ref.at[:, pl.ds(offset, rows)], held, sem)
        load.start()
        load.wait()

        def copy(u):
            return pltpu.make_async_copy(held.at[u], out_ref.at[position_ref[u]], sems.at[u])

        for u in range(count):
            copy(u).start()
        for u in range(count):
            copy(u).wait()

    return pl.pallas_call(
        body,
        out_shape=jax.ShapeDtypeStruct((cells, rows, width), pieces.dtype),
        in_specs=[pl.BlockSpec(memory_space=pltpu.SMEM), pl.BlockSpec(memory_space=pl.ANY)],
        out_specs=pl.BlockSpec(memory_space=pl.ANY),
        scratch_shapes=[
            pltpu.VMEM((count, rows, width), pieces.dtype),
            pltpu.SemaphoreType.DMA,
            pltpu.SemaphoreType.DMA((count,)),
        ],
        compiler_params=pltpu.CompilerParams(vmem_limit_bytes=KERNEL_VMEM),
        cost_estimate=pl.CostEstimate(flops=0, bytes_accessed=4 * count * rows * width, transcendentals=0),
        name="pick_rows",
    )(position, pieces)


def gather_rows(position, cells):
    count = position.shape[0]
    _, rows, width = cells.shape

    def body(position_ref, cells_ref, out_ref, held, sem, sems):
        def copy(t):
            return pltpu.make_async_copy(cells_ref.at[position_ref[t]], held.at[t], sems.at[t])

        for t in range(count):
            copy(t).start()
        for t in range(count):
            copy(t).wait()
        store = pltpu.make_async_copy(held, out_ref, sem)
        store.start()
        store.wait()

    return pl.pallas_call(
        body,
        out_shape=jax.ShapeDtypeStruct((count, rows, width), cells.dtype),
        in_specs=[pl.BlockSpec(memory_space=pltpu.SMEM), pl.BlockSpec(memory_space=pl.ANY)],
        out_specs=pl.BlockSpec(memory_space=pl.ANY),
        scratch_shapes=[
            pltpu.VMEM((count, rows, width), cells.dtype),
            pltpu.SemaphoreType.DMA,
            pltpu.SemaphoreType.DMA((count,)),
        ],
        compiler_params=pltpu.CompilerParams(vmem_limit_bytes=KERNEL_VMEM),
        cost_estimate=pl.CostEstimate(flops=0, bytes_accessed=4 * count * rows * width, transcendentals=0),
        name="place_rows",
    )(position, cells)


def after(x, *others):
    return lax.optimization_barrier((x,) + others)[0]


def send(x, step):
    size = lax.axis_size("tp")
    return lax.ppermute(x, "tp", [(i, (i + step) % size) for i in range(size)])


def project(parts, gain, key_matrix, value_matrix):
    if parts[-1][0] is None:
        parts = parts[1:]
    rows, width = parts[0][2].shape[-2:]
    depth, columns = key_matrix.shape
    size = depth // width
    tile = 256
    block = 16
    here = lax.axis_index("tp").astype(jnp.int32).reshape(1)
    n = len(parts)

    def body(here_ref, gain_ref, key_ref, value_ref, *refs):
        part_refs, key_out, value_out, encoded = refs[:n], refs[n], refs[n + 1], refs[n + 2]

        @pl.when(pl.program_id(0) == 0)
        def _():
            def group(first, last, some):
                def load(ref, at, start):
                    return ref[pl.ds(pl.multiple_of(at - start, block), block), :].astype(jnp.float32)

                def place_of(step):
                    if isinstance(step, tuple):
                        return slice(step[0] * width, (step[0] + 1) * width)
                    return pl.ds(pl.multiple_of((here_ref[0] + step) % size * width, width), width)

                @pl.loop(0, (last - first) // block, unroll=2)
                def _(b):
                    at = pl.multiple_of(first + b * block, block)
                    total = jnp.zeros((block, HD), jnp.float32)
                    for _, start, ref in some:
                        x = load(ref, at, start)
                        for c in range(0, width, HD):
                            total = total + x[:, c : c + HD] * x[:, c : c + HD]
                    total = jnp.sum(total, -1, keepdims=True)
                    scale = lax.rsqrt(total * (1.0 / depth) + EPS)
                    for step, start, ref in some:
                        chunk = place_of(step)
                        encoded[pl.ds(at, block), chunk] = (
                            load(ref, at, start) * scale * gain_ref[:, chunk]
                        ).astype(jnp.bfloat16)

            refs_of = [(step, start, ref) for (step, start, _), ref in zip(parts, part_refs)]
            if parts[0][0] is None:
                refs_of = [((p,), 0, part_refs[0].at[p]) for p in range(size)]
            edges = sorted({0, rows} | {start for _, start, _ in refs_of})
            for first, last in zip(edges, edges[1:]):
                group(first, last, [r for r in refs_of if r[1] <= first and last <= r[1] + r[2].shape[0]])

        rows_now = encoded[...]
        key_out[...] = jnp.dot(rows_now, key_ref[...], preferred_element_type=jnp.float32).astype(jnp.bfloat16)
        value_out[...] = jnp.dot(rows_now, value_ref[...], preferred_element_type=jnp.float32).astype(jnp.bfloat16)

    out = jax.ShapeDtypeStruct((rows, columns), jnp.bfloat16)
    return pl.pallas_call(
        body,
        grid=(columns // tile,),
        out_shape=(out, out),
        in_specs=[
            pl.BlockSpec(memory_space=pltpu.SMEM),
            pl.BlockSpec((1, depth), lambda i: (0, 0)),
            pl.BlockSpec((depth, tile), lambda i: (0, i)),
            pl.BlockSpec((depth, tile), lambda i: (0, i)),
        ]
        + [pl.BlockSpec(x.shape, lambda i, n=x.ndim: (0,) * n) for _, _, x in parts],
        out_specs=(pl.BlockSpec((rows, tile), lambda i: (0, i)), pl.BlockSpec((rows, tile), lambda i: (0, i))),
        scratch_shapes=[pltpu.VMEM((rows, depth), jnp.bfloat16)],
        compiler_params=pltpu.CompilerParams(vmem_limit_bytes=KERNEL_VMEM),
        cost_estimate=pl.CostEstimate(
            flops=4 * rows * depth * columns, bytes_accessed=4 * depth * columns + 2 * rows * depth, transcendentals=0
        ),
        name="norm_and_project",
    )(here, gain.reshape(1, depth), key_matrix, value_matrix, *[x for _, _, x in parts])


def attend(queries, keys, values, counts):
    stretches = counts.shape[0]
    tokens, width = queries.shape
    stretch = tokens // stretches
    heads = width // HD
    spans = [k.shape[1] for k in keys]
    span = sum(spans)
    n = len(keys)

    per = 2

    def body(count_ref, query_ref, *refs):
        key_refs, value_refs, out_ref = refs[:n], refs[n : 2 * n], refs[2 * n]
        column = lax.broadcasted_iota(jnp.int32, (1, span), 1)
        neighbour = jnp.zeros((1, span), jnp.int32)
        start = 0
        for s in spans:
            for k in range(1, NBR):
                low = start + k * (s // NBR)
                neighbour = jnp.where((column >= low) & (column < low + s // NBR), k, neighbour)
            start += s
        at = [slice(h * HD, (h + 1) * HD) for h in range(heads)]
        for c in range(per):
            row = slice(c * stretch, (c + 1) * stretch)
            kept = neighbour < count_ref[pl.program_id(0) * per + c]
            scores = []
            for a in at:
                k = jnp.concatenate([r[c, :, a] for r in key_refs], 0)
                scores.append(
                    lax.dot_general(
                        query_ref[row, a], k, (((1,), (1,)), ((), ())), preferred_element_type=jnp.float32
                    )
                )
            scores = jnp.concatenate(scores, 0) * HD ** (-0.5)
            scores = jnp.where(kept, scores, -1e30)
            exponents = jnp.exp(scores - jnp.max(scores, -1, keepdims=True))
            weights = (exponents / jnp.sum(exponents, -1, keepdims=True)).astype(jnp.bfloat16)
            for h, a in enumerate(at):
                v = jnp.concatenate([r[c, :, a] for r in value_refs], 0)
                out_ref[row, a] = jnp.dot(
                    weights[h * stretch : (h + 1) * stretch], v, preferred_element_type=jnp.float32
                ).astype(jnp.bfloat16)

    return pl.pallas_call(
        body,
        grid=(stretches // per,),
        out_shape=jax.ShapeDtypeStruct(queries.shape, queries.dtype),
        in_specs=[pl.BlockSpec(memory_space=pltpu.SMEM), pl.BlockSpec((per * stretch, width), lambda c: (c, 0))]
        + [pl.BlockSpec((per, s, width), lambda c: (c, 0, 0)) for s in spans + spans],
        out_specs=pl.BlockSpec((per * stretch, width), lambda c: (c, 0)),
        compiler_params=pltpu.CompilerParams(vmem_limit_bytes=KERNEL_VMEM),
        cost_estimate=pl.CostEstimate(
            flops=4 * tokens * span * width, bytes_accessed=4 * (tokens + stretches * span) * width, transcendentals=tokens * span * heads
        ),
        name="attention",
    )(counts, queries, *keys, *values)


def per_device(queries, neighbours, norm_gain, key_weight, value_weight, slot_anchor, nbr_count):
    owners = lax.axis_size("section") * lax.axis_size("seq")
    slot_count = slot_anchor.shape[0]
    stretches = nbr_count.shape[0]
    width_part = neighbours.shape[1]
    capacity = 2 * ((slot_count // 2 + owners - 1) // owners)
    cells = owners * capacity

    source = slot_anchor // slot_count
    unit_index = slot_anchor % slot_count
    earlier = (source[None, :] == source[:, None]) & (slot_anchor[None, :] < slot_anchor[:, None])
    rank_among = jnp.sum(earlier.astype(jnp.int32), 1)
    grid_cell = source * capacity + rank_among
    cell_ids = jnp.arange(cells, dtype=jnp.int32)
    cell_match = grid_cell[None, :] == cell_ids[:, None]
    request = jnp.sum(jnp.where(cell_match, unit_index[None, :] + 1, 0), 1) - 1
    asked = lax.all_to_all(
        request.reshape(owners, capacity), OWN, split_axis=0, concat_axis=0, tiled=True
    ).reshape(cells)
    units = jnp.arange(slot_count, dtype=jnp.int32)
    position = jnp.max(jnp.where(asked[None, :] == units[:, None], cell_ids[None, :], 0), 1)

    pieces = neighbours.reshape(slot_count, PIECE, width_part)
    starts = [sum(CHUNKS[:j]) for j in range(len(CHUNKS))]
    count = len(CHUNKS)
    size = lax.axis_size("tp")

    def pick(j):
        return scatter_rows(position, pieces, starts[j], CHUNKS[j], cells).reshape(
            owners, capacity, CHUNKS[j], width_part
        )

    def place(j, arrived):
        return gather_rows(grid_cell, arrived.reshape(cells, CHUNKS[j], width_part)).reshape(-1, width_part)

    def shape_rows(x):
        return x.reshape(stretches, -1, x.shape[1])

    parts, done, halves = [], {}, {}

    def finish(j):
        done[j] = project(parts[j], norm_gain, key_weight[0], value_weight[0])

    picked = [pick(j) for j in range(count)]
    for j in range(count):
        ready = picked[j]
        if j >= 2:
            ready = after(ready, parts[j - 2][0][2])
        arrived = lax.all_to_all(ready, OWN, split_axis=0, concat_axis=0, tiled=True)
        if j == 0:
            arrived = after(arrived, *picked[1:])
        if j >= 3:
            finish(j - 3)
            arrived = after(arrived, done[j - 3][0])
        if j - 1 in halves:
            arrived = after(arrived, *halves[j - 1])
        own = place(j, arrived)
        if MODE[j] == "offload":
            full = lax.all_gather(own, "tp", axis=0)
            parts.append([(0, 0, own), (None, 0, full)])
            continue
        up, down = send(own, 1), send(own, size - 1)
        half = own.shape[0] // 2
        halves[j] = up[:half], down[half:]
        far = send(halves[j][0], 1), send(halves[j][1], size - 1)
        parts.append([(0, 0, own), (size - 1, 0, up), (1, 0, down), (2, 0, far[0]), (2, half, far[1])])
    parts[-2][-1] = parts[-2][-1][:2] + (after(parts[-2][-1][2], *halves[count - 1]),)
    parts[-3][-1] = parts[-3][-1][:2] + (after(parts[-3][-1][2], parts[-1][0][2]),)
    for j in range(count):
        if j not in done:
            finish(j)
    keys = [done[j][0] for j in range(count)]
    values = [done[j][1] for j in range(count)]
    keys = [shape_rows(x) for x in keys]
    values = [shape_rows(x) for x in values]
    return attend(queries, keys, values, nbr_count)


def solution(mesh):
    in_specs = (
        P(("section", "seq"), "tp"),
        P(("section", "seq"), "tp"),
        P(),
        P("section", None, "tp"),
        P("section", None, "tp"),
        P(("section", "seq")),
        P(("section", "seq")),
    )
    out_specs = P(("section", "seq"), "tp")
    return jax.shard_map(
        per_device, mesh=mesh, in_specs=in_specs, out_specs=out_specs, check_vma=False
    )
```

time: 328 us -> 247 us (0.75)
  waiting for transfers between devices: 220 us -> 82.4 us
  Pallas kernels: 0 us -> 85.9 us
  matrix products: 37.6 us -> 0 us
  starting transfers between devices: 6.09 us -> 41.3 us
  other arithmetic: 20.4 us -> 3.01 us
  local copies, waits for them, and re-layouts: 16 us -> 5.74 us
    all_gather x1 -> x2, waiting for transfers between devices: 120 us -> 0.01 us  [per_device(): full = lax.all_gather(own, 'tp', axis=0)]
    pallas_call x0 -> x13, Pallas kernels: none -> 85.9 us  [the longest x4 56.4 us: project(): pl.pallas_call(body, grid=(columns // tile,), out_shape=(out, out), in_sp...]
    all_to_all x1 -> x4, waiting for transfers between devices: 99.5 us -> 58.6 us  [per_device(): lax.all_to_all(ready, OWN, split_axis=0, concat_axis=0, tiled=True)]
    dot_general x4 -> x0, matrix products: 37.6 us -> none  [the longest x1 18.7 us: per_device(): jnp.dot(encoded, value_matrix, preferred_element_type=jnp.float32)]
    ppermute x0 -> x8, waiting for transfers between devices: none -> 23.7 us  [send(): return lax.ppermute(x, 'tp', [(i, (i + step) % size) for i in range(size)])]
    all_to_all x1 -> x4, starting transfers between devices: 6.05 us -> 25.3 us  [per_device(): lax.all_to_all(ready, OWN, split_axis=0, concat_axis=0, tiled=True)]
    ppermute x0 -> x8, starting transfers between devices: none -> 15.9 us  [send(): return lax.ppermute(x, 'tp', [(i, (i + step) % size) for i in range(size)])]
    select_n x6 -> x0, other arithmetic: 10.6 us -> none  [the longest x1 7.62 us: per_device(): jnp.where((asked_units >= 0)[:, :, None, None], picked, jnp.zeros_like(pi...]
  transfers between devices with their start and end apart: 2 -> 14, of which waited for: 2 -> 6; matrix products, arithmetic and copies ran while one was open for 0% -> 1% of each run, Pallas kernels for 0% -> 24%
where the time goes in v1:
time: 247 us; the launch traced here: 245 us
  Pallas kernels  85.9 us (35%)
  waiting for transfers between devices  82.4 us (33%)
  starting transfers between devices  41.3 us (17%)
  blocking collectives  13.6 us (6%)
  between operations  13.6 us (6%)
  local copies, waits for them, and re-layouts  5.74 us (2%)
  other arithmetic  3.01 us (1%)
    all_to_all x4, waiting for transfers between devices, per_device(): lax.all_to_all(ready, OWN, split_axis=0, concat_axis=0, tiled=True)  58.6 us
    pallas_call x4, Pallas kernels, project(): pl.pallas_call(body, grid=(columns // tile,), out_shape=(out, out), in_sp...  56.4 us
    all_to_all x4, starting transfers between devices, per_device(): lax.all_to_all(ready, OWN, split_axis=0, concat_axis=0, tiled=True)  25.3 us
    ppermute x8, waiting for transfers between devices, send(): return lax.ppermute(x, 'tp', [(i, (i + step) % size) for i in range(size)])  23.7 us
    ppermute x8, starting transfers between devices, send(): return lax.ppermute(x, 'tp', [(i, (i + step) % size) for i in range(size)])  15.9 us
    all_to_all x1, blocking collectives, per_device(): lax.all_to_all(request.reshape(owners, capacity), OWN, split_axis=0, conc...  13.6 us
    pallas_call x4, Pallas kernels, scatter_rows(): pl.pallas_call(body, out_shape=jax.ShapeDtypeStruct((cells, rows, width),...  11.8 us
    pallas_call x4, Pallas kernels, gather_rows(): pl.pallas_call(body, out_shape=jax.ShapeDtypeStruct((count, rows, width),...  11.5 us
  transfers between devices with their start and end apart: 14, of which 6 were waited for; matrix products, arithmetic and copies ran while one was open for 1% of the time, Pallas kernels for 24%

profile of v1, /device:TPU:2, one launch (start us, length us, event | category | flops | bytes accessed | tf_op | source)
XLA Modules:
  0.0 245.5 jit_solution(15656869975822616669)
XLA Ops:
  8.3 13.6 %all_to_all.26 = s32[32,1,2]{2,1,0:T(1,128)S(1)} all-to-all(s32[32,1,2]{2,1,0:T(1,128)S(1)} %bitcast.50), channel_id=1, replica_groups=mesh['section'=4,'seq'=8,'tp'=4] {'section','seq'}, dimensions={0} | all-to-all | bytes 512 | tf_op jit(solution)/shard_map/all_to_all | solution.py:241
  23.8 2.9 %pick_rows.4 = bf16[64,16,1024]{2,1,0:T(8,128)(2,1)} custom-call(s32[24]{0:T(128)} %select_reduce_fusion.position_ref, bf16[24,64,1024]{2,1,0:T(8,128)(2,1)} %bitcast.26), custom_call_target="tpu_custom_call" | custom-call | bytes 1572864 | tf_op jit(solution)/shard_map/pick_rows/pallas_call | solution.py:36
  26.8 5.8 %all-to-all-start.1 = ((bf16[32,2,16,1024]{3,2,1,0:T(8,128)(2,1)}), bf16[32,2,16,1024]{3,2,1,0:T(8,128)(2,1)}, u32[]{:S(2)}, u32[]{:S(2)}) async-start(bf16[32,2,16,1024]{3,2,1,0:T(8,128)(2,1)} %bitcast.33), calls=%async_computation.1 | async-start | bytes 4194304 | tf_op jit(solution)/shard_map/all_to_all | solution.py:273
  32.7 3.0 %pick_rows.5 = bf16[64,16,1024]{2,1,0:T(8,128)(2,1)} custom-call(s32[24]{0:T(128)} %select_reduce_fusion.position_ref, bf16[24,64,1024]{2,1,0:T(8,128)(2,1)} %bitcast.27), custom_call_target="tpu_custom_call" | custom-call | bytes 1572864 | tf_op jit(solution)/shard_map/pick_rows/pallas_call | solution.py:36
  35.7 2.9 %pick_rows.6 = bf16[64,16,1024]{2,1,0:T(8,128)(2,1)} custom-call(s32[24]{0:T(128)} %select_reduce_fusion.position_ref, bf16[24,64,1024]{2,1,0:T(8,128)(2,1)} %bitcast.28), custom_call_target="tpu_custom_call" | custom-call | bytes 1572864 | tf_op jit(solution)/shard_map/pick_rows/pallas_call | solution.py:36
  38.6 2.9 %pick_rows.7 = bf16[64,16,1024]{2,1,0:T(8,128)(2,1)} custom-call(s32[24]{0:T(128)} %select_reduce_fusion.position_ref, bf16[24,64,1024]{2,1,0:T(8,128)(2,1)} %bitcast.29), custom_call_target="tpu_custom_call" | custom-call | bytes 1572864 | tf_op jit(solution)/shard_map/pick_rows/pallas_call | solution.py:36
  41.5 19.1 %all-to-all-done.1 = bf16[32,2,16,1024]{3,2,1,0:T(8,128)(2,1)} async-done(((bf16[32,2,16,1024]{3,2,1,0:T(8,128)(2,1)}), bf16[32,2,16,1024]{3,2,1,0:T(8,128)(2,1)}, u32[]{:S(2)}, u32[]{:S(2)}) %all-to-all-start.1) | async-done | bytes 2097184 | tf_op jit(solution)/shard_map/all_to_all | solution.py:273
  60.6 2.8 %place_rows.4 = bf16[24,16,1024]{2,1,0:T(8,128)(2,1)} custom-call(s32[24]{0:T(128)} %copy-done.4, bf16[64,16,1024]{2,1,0:T(8,128)(2,1)} %bitcast.10.cells_ref), custom_call_target="tpu_custom_call" | custom-call | bytes 1572864 | tf_op jit(solution)/shard_map/place_rows/pallas_call | solution.py:68
  63.5 6.0 %all-to-all-start.2 = ((bf16[32,2,16,1024]{3,2,1,0:T(8,128)(2,1)}), bf16[32,2,16,1024]{3,2,1,0:T(8,128)(2,1)S(1)}, u32[]{:S(2)}, u32[]{:S(2)}) async-start(bf16[32,2,16,1024]{3,2,1,0:T(8,128)(2,1)} %bitcast.31), calls=%async_computation.2 | async-start | bytes 4194304 | tf_op jit(solution)/shard_map/all_to_all | solution.py:273
  69.6 28.0 %all-to-all-done.2 = bf16[32,2,16,1024]{3,2,1,0:T(8,128)(2,1)S(1)} async-done(((bf16[32,2,16,1024]{3,2,1,0:T(8,128)(2,1)}), bf16[32,2,16,1024]{3,2,1,0:T(8,128)(2,1)S(1)}, u32[]{:S(2)}, u32[]{:S(2)}) %all-to-all-start.2) | async-done | bytes 2097184 | tf_op jit(solution)/shard_map/all_to_all | solution.py:273
  97.5 1.3 copy-done
  98.9 6.7 %all-to-all-start.4 = ((bf16[32,2,16,1024]{3,2,1,0:T(8,128)(2,1)}), bf16[32,2,16,1024]{3,2,1,0:T(8,128)(2,1)}, u32[]{:S(2)}, u32[]{:S(2)}) async-start(bf16[32,2,16,1024]{3,2,1,0:T(8,128)(2,1)} %bitcast.8), calls=%async_computation.4 | async-start | bytes 4194304 | tf_op jit(solution)/shard_map/all_to_all | solution.py:273
  105.6 2.9 %place_rows.5 = bf16[24,16,1024]{2,1,0:T(8,128)(2,1)} custom-call(s32[24]{0:T(128)} %copy-done.4, bf16[64,16,1024]{2,1,0:T(8,128)(2,1)} %bitcast.32), custom_call_target="tpu_custom_call" | custom-call | bytes 1572864 | tf_op jit(solution)/shard_map/place_rows/pallas_call | solution.py:68
  108.5 2.0 collective-permute-start
  110.5 2.2 collective-permute-start.1
  112.7 18.0 %collective-permute-done.refs_1_ = bf16[384,1024]{1,0:T(8,128)(2,1)S(1)} collective-permute-done((bf16[384,1024]{1,0:T(8,128)(2,1)}, bf16[384,1024]{1,0:T(8,128)(2,1)S(1)}, u32[]{:S(2)}, u32[]{:S(2)}) %collective-permute-start) | collective-permute-done | bytes 786464 | tf_op jit(solution)/shard_map/ppermute | solution.py:90
  131.7 1.9 all-to-all-done.4
  133.6 2.9 %place_rows.7 = bf16[24,16,1024]{2,1,0:T(8,128)(2,1)} custom-call(s32[24]{0:T(128)} %copy-done.4, bf16[64,16,1024]{2,1,0:T(8,128)(2,1)} %bitcast.18.cells_ref), custom_call_target="tpu_custom_call" | custom-call | bytes 1572864 | tf_op jit(solution)/shard_map/place_rows/pallas_call | solution.py:68
  136.5 6.7 %all-to-all-start.3 = ((bf16[32,2,16,1024]{3,2,1,0:T(8,128)(2,1)}), bf16[32,2,16,1024]{3,2,1,0:T(8,128)(2,1)}, u32[]{:S(2)}, u32[]{:S(2)}) async-start(bf16[32,2,16,1024]{3,2,1,0:T(8,128)(2,1)} %bitcast.30), calls=%async_computation.3 | async-start | bytes 4194304 | tf_op jit(solution)/shard_map/all_to_all | solution.py:273
  143.3 2.0 collective-permute-start.2
  145.2 2.2 collective-permute-start.3
  147.5 14.2 %norm_and_project.4 = (bf16[384,1024]{1,0:T(8,128)(2,1)}, bf16[384,1024]{1,0:T(8,128)(2,1)}) custom-call(s32[1]{0:T(128)} %bitcast.here_ref, f32[1,4096]{1,0:T(1,128)} %bitcast.59, bf16[4096,1024]{1,0:T(8,128)(2,1)} %bitcast.51, bf16[4096,1024]{1,0:T(8,128)(2,1)} %bitcast.55, bf16[4,384,1024]{2,1,0:T(8,128)(2,1)} %all-gather.3.cloned.1.call-done.refs_0_), custom_call_target="tpu_custom_call" | custom-call | flops 6442450944 | bytes 19922944 | tf_op jit(solution)/shard_map/norm_and_project/pallas_call | solution.py:146
  161.6 9.6 %all-to-all-done.3 = bf16[32,2,16,1024]{3,2,1,0:T(8,128)(2,1)} async-done(((bf16[32,2,16,1024]{3,2,1,0:T(8,128)(2,1)}), bf16[32,2,16,1024]{3,2,1,0:T(8,128)(2,1)}, u32[]{:S(2)}, u32[]{:S(2)}) %all-to-all-start.3) | async-done | bytes 2097184 | tf_op jit(solution)/shard_map/all_to_all | solution.py:273
  171.3 2.9 %place_rows.6 = bf16[24,16,1024]{2,1,0:T(8,128)(2,1)} custom-call(s32[24]{0:T(128)} %copy-done.4, bf16[64,16,1024]{2,1,0:T(8,128)(2,1)} %bitcast.15.cells_ref), custom_call_target="tpu_custom_call" | custom-call | bytes 1572864 | tf_op jit(solution)/shard_map/place_rows/pallas_call | solution.py:68
  174.2 2.0 collective-permute-start.4
  176.1 2.2 collective-permute-start.5
  179.1 14.1 %norm_and_project.5 = (bf16[384,1024]{1,0:T(8,128)(2,1)}, bf16[384,1024]{1,0:T(8,128)(2,1)}) custom-call(s32[1]{0:T(128)} %bitcast.here_ref, f32[1,4096]{1,0:T(1,128)} %bitcast.60, bf16[4096,1024]{1,0:T(8,128)(2,1)} %bitcast.52, bf16[4096,1024]{1,0:T(8,128)(2,1)} %bitcast.56, bf16[384,1024]{1,0:T(8,128)(2,1)} %bitcast.38, bf16[384,1024]{1,0:T(8,128)(2,1)} %copy-done.1, ...), custom_call_target="tpu_custom_call" | custom-call | flops 6442450944 | bytes 19922944 | tf_op jit(solution)/shard_map/norm_and_project/pallas_call | solution.py:146
  193.2 5.7 %collective-permute-done.4.refs_1_ = bf16[384,1024]{1,0:T(8,128)(2,1)S(1)} collective-permute-done((bf16[384,1024]{1,0:T(8,128)(2,1)}, bf16[384,1024]{1,0:T(8,128)(2,1)S(1)}, u32[]{:S(2)}, u32[]{:S(2)}) %collective-permute-start.4) | collective-permute-done | bytes 786464 | tf_op jit(solution)/shard_map/ppermute | solution.py:90
  200.2 3.3 %collective-permute-start.7 = (bf16[192,1024]{1,0:T(8,128)(2,1)S(1)}, bf16[192,1024]{1,0:T(8,128)(2,1)}, u32[]{:S(2)}, u32[]{:S(2)}) collective-permute-start(bf16[192,1024]{1,0:T(8,128)(2,1)S(1)} %slice.19), channel_id=1, source_target_pairs={{0,3},{1,0},{2,1},{3,2},{4,7},{5,4},{6,5},{7,6},{8,11},{9,8},{10,9... | collective-permute-start | bytes 1179656 | tf_op jit(solution)/shard_map/ppermute | solution.py:90
  203.5 14.1 %norm_and_project.6 = (bf16[384,1024]{1,0:T(8,128)(2,1)}, bf16[384,1024]{1,0:T(8,128)(2,1)}) custom-call(s32[1]{0:T(128)} %bitcast.here_ref, f32[1,4096]{1,0:T(1,128)} %bitcast.61, bf16[4096,1024]{1,0:T(8,128)(2,1)} %bitcast.53, bf16[4096,1024]{1,0:T(8,128)(2,1)} %bitcast.57, bf16[4,384,1024]{2,1,0:T(8,128)(2,1)} %all-gather.5.cloned.1.call-done.refs_0_), custom_call_target="tpu_custom_call" | custom-call | flops 6442450944 | bytes 19922944 | tf_op jit(solution)/shard_map/norm_and_project/pallas_call | solution.py:146
  218.4 14.0 %norm_and_project.7 = (bf16[384,1024]{1,0:T(8,128)(2,1)}, bf16[384,1024]{1,0:T(8,128)(2,1)}) custom-call(s32[1]{0:T(128)} %bitcast.here_ref, f32[1,4096]{1,0:T(1,128)} %bitcast.62, bf16[4096,1024]{1,0:T(8,128)(2,1)} %bitcast.54, bf16[4096,1024]{1,0:T(8,128)(2,1)} %bitcast.58, bf16[384,1024]{1,0:T(8,128)(2,1)} %bitcast.41, bf16[384,1024]{1,0:T(8,128)(2,1)} %copy-done.3, ...), custom_call_target="tpu_custom_call" | custom-call | flops 6442450944 | bytes 19922944 | tf_op jit(solution)/shard_map/norm_and_project/pallas_call | solution.py:146
  232.4 6.2 %attention.1 = bf16[384,1024]{1,0:T(8,128)(2,1)} custom-call(s32[6]{0:T(128)} %count_ref.1, bf16[384,1024]{1,0:T(8,128)(2,1)} %query_ref.1, bf16[6,64,1024]{2,1,0:T(8,128)(2,1)} %bitcast.42, bf16[6,64,1024]{2,1,0:T(8,128)(2,1)} %bitcast.44, bf16[6,64,1024]{2,1,0:T(8,128)(2,1)} %bitcast.46, bf16[6,64,1024]{2,1,0:T(8,128)(2,1)} %bitcast.48, ...), custom_call_target="tpu_custom_call" | custom-call | flops 402653184 | bytes 7864320 | tf_op jit(solution)/shard_map/attention/pallas_call | solution.py:210
  (40 shorter events, 7.6 us)
Async XLA Ops:
  8.1 18.7 %copy-start.4 = (s32[24]{0:T(128)}, s32[24]{0:T(128)S(1)}, u32[]{:S(2)}) copy-start(s32[24]{0:T(128)S(1)} %multiply_add_fusion.position_ref) | copy-start | bytes 292
  26.8 33.8 %all-to-all-start.1 = ((bf16[32,2,16,1024]{3,2,1,0:T(8,128)(2,1)}), bf16[32,2,16,1024]{3,2,1,0:T(8,128)(2,1)}, u32[]{:S(2)}, u32[]{:S(2)}) async-start(bf16[32,2,16,1024]{3,2,1,0:T(8,128)(2,1)} %bitcast.33), calls=%async_computation.1 | async-start | bytes 4194304 | tf_op jit(solution)/shard_map/all_to_all | solution.py:273
  32.6 114.8 %all-gather.3.cloned.1.call-start = ((), (), s32[]{:S(2)}) async-start(), calls=%async_computation.5 | async-start | bytes 3932160 | tf_op jit(solution)/shard_map/all_gather | solution.py:283
  63.5 34.0 %all-to-all-start.2 = ((bf16[32,2,16,1024]{3,2,1,0:T(8,128)(2,1)}), bf16[32,2,16,1024]{3,2,1,0:T(8,128)(2,1)S(1)}, u32[]{:S(2)}, u32[]{:S(2)}) async-start(bf16[32,2,16,1024]{3,2,1,0:T(8,128)(2,1)} %bitcast.31), calls=%async_computation.2 | async-start | bytes 4194304 | tf_op jit(solution)/shard_map/all_to_all | solution.py:273
  97.5 1.3 copy-start
  98.9 34.7 %all-to-all-start.4 = ((bf16[32,2,16,1024]{3,2,1,0:T(8,128)(2,1)}), bf16[32,2,16,1024]{3,2,1,0:T(8,128)(2,1)}, u32[]{:S(2)}, u32[]{:S(2)}) async-start(bf16[32,2,16,1024]{3,2,1,0:T(8,128)(2,1)} %bitcast.8), calls=%async_computation.4 | async-start | bytes 4194304 | tf_op jit(solution)/shard_map/all_to_all | solution.py:273
  105.6 98.0 %all-gather.5.cloned.1.call-start = ((), (), s32[]{:S(2)}) async-start(), calls=%async_computation.6 | async-start | bytes 3932160 | tf_op jit(solution)/shard_map/all_gather | solution.py:283
  108.5 22.2 %collective-permute-start = (bf16[384,1024]{1,0:T(8,128)(2,1)}, bf16[384,1024]{1,0:T(8,128)(2,1)S(1)}, u32[]{:S(2)}, u32[]{:S(2)}) collective-permute-start(bf16[384,1024]{1,0:T(8,128)(2,1)} %bitcast.36), channel_id=1, source_target_pairs={{0,1},{1,2},{2,3},{3,0},{4,5},{5,6},{6,7},{7,4},{8,9},{9,10},{10,1... | collective-permute-start | bytes 2359304 | tf_op jit(solution)/shard_map/ppermute | solution.py:90
  110.5 20.2 %collective-permute-start.1 = (bf16[384,1024]{1,0:T(8,128)(2,1)}, bf16[384,1024]{1,0:T(8,128)(2,1)S(1)}, u32[]{:S(2)}, u32[]{:S(2)}) collective-permute-start(bf16[384,1024]{1,0:T(8,128)(2,1)} %bitcast.37), channel_id=1, source_target_pairs={{0,3},{1,0},{2,1},{3,2},{4,7},{5,4},{6,5},{7,6},{8,11},{9,8},{10,9... | collective-permute-start | bytes 2359304 | tf_op jit(solution)/shard_map/ppermute | solution.py:90
  130.7 5.8 %copy-start.1 = (bf16[384,1024]{1,0:T(8,128)(2,1)}, bf16[384,1024]{1,0:T(8,128)(2,1)S(1)}, u32[]{:S(2)}) copy-start(bf16[384,1024]{1,0:T(8,128)(2,1)S(1)} %collective-permute-done.refs_1_) | copy-start | bytes 2359300
  130.7 0.9 copy-start.2
  136.5 34.7 %all-to-all-start.3 = ((bf16[32,2,16,1024]{3,2,1,0:T(8,128)(2,1)}), bf16[32,2,16,1024]{3,2,1,0:T(8,128)(2,1)}, u32[]{:S(2)}, u32[]{:S(2)}) async-start(bf16[32,2,16,1024]{3,2,1,0:T(8,128)(2,1)} %bitcast.30), calls=%async_computation.3 | async-start | bytes 4194304 | tf_op jit(solution)/shard_map/all_to_all | solution.py:273
  143.3 35.1 %collective-permute-start.2 = (bf16[192,1024]{1,0:T(8,128)(2,1)S(1)}, bf16[192,1024]{1,0:T(8,128)(2,1)S(1)}, u32[]{:S(2)}, u32[]{:S(2)}) collective-permute-start(bf16[192,1024]{1,0:T(8,128)(2,1)S(1)} %slice.16), channel_id=1, source_target_pairs={{0,1},{1,2},{2,3},{3,0},{4,5},{5,6},{6,7},{7,4},{8,9},{9,10},{10,1... | collective-permute-start | bytes 1179656 | tf_op jit(solution)/shard_map/ppermute | solution.py:90
  145.2 33.1 %collective-permute-start.3 = (bf16[192,1024]{1,0:T(8,128)(2,1)S(1)}, bf16[192,1024]{1,0:T(8,128)(2,1)}, u32[]{:S(2)}, u32[]{:S(2)}) collective-permute-start(bf16[192,1024]{1,0:T(8,128)(2,1)S(1)} %slice.17), channel_id=1, source_target_pairs={{0,3},{1,0},{2,1},{3,2},{4,7},{5,4},{6,5},{7,6},{8,11},{9,8},{10,9... | collective-permute-start | bytes 1179656 | tf_op jit(solution)/shard_map/ppermute | solution.py:90
  174.2 24.8 %collective-permute-start.4 = (bf16[384,1024]{1,0:T(8,128)(2,1)}, bf16[384,1024]{1,0:T(8,128)(2,1)S(1)}, u32[]{:S(2)}, u32[]{:S(2)}) collective-permute-start(bf16[384,1024]{1,0:T(8,128)(2,1)} %bitcast.39), channel_id=1, source_target_pairs={{0,1},{1,2},{2,3},{3,0},{4,5},{5,6},{6,7},{7,4},{8,9},{9,10},{10,1... | collective-permute-start | bytes 2359304 | tf_op jit(solution)/shard_map/ppermute | solution.py:90
  176.1 22.9 %collective-permute-start.5 = (bf16[384,1024]{1,0:T(8,128)(2,1)}, bf16[384,1024]{1,0:T(8,128)(2,1)}, u32[]{:S(2)}, u32[]{:S(2)}) collective-permute-start(bf16[384,1024]{1,0:T(8,128)(2,1)} %bitcast.40), channel_id=1, source_target_pairs={{0,3},{1,0},{2,1},{3,2},{4,7},{5,4},{6,5},{7,6},{8,11},{9,8},{10,9... | collective-permute-start | bytes 2359304 | tf_op jit(solution)/shard_map/ppermute | solution.py:90
  178.3 0.8 copy-start.5
  198.9 18.7 %copy-start.3 = (bf16[384,1024]{1,0:T(8,128)(2,1)}, bf16[384,1024]{1,0:T(8,128)(2,1)S(1)}, u32[]{:S(2)}) copy-start(bf16[384,1024]{1,0:T(8,128)(2,1)S(1)} %collective-permute-done.4.refs_1_) | copy-start | bytes 2359300
  199.0 18.7 %collective-permute-start.6 = (bf16[192,1024]{1,0:T(8,128)(2,1)S(1)}, bf16[192,1024]{1,0:T(8,128)(2,1)S(1)}, u32[]{:S(2)}, u32[]{:S(2)}) collective-permute-start(bf16[192,1024]{1,0:T(8,128)(2,1)S(1)} %slice.18), channel_id=1, source_target_pairs={{0,1},{1,2},{2,3},{3,0},{4,5},{5,6},{6,7},{7,4},{8,9},{9,10},{10,1... | collective-permute-start | bytes 1179656 | tf_op jit(solution)/shard_map/ppermute | solution.py:90
  200.2 17.4 %collective-permute-start.7 = (bf16[192,1024]{1,0:T(8,128)(2,1)S(1)}, bf16[192,1024]{1,0:T(8,128)(2,1)}, u32[]{:S(2)}, u32[]{:S(2)}) collective-permute-start(bf16[192,1024]{1,0:T(8,128)(2,1)S(1)} %slice.19), channel_id=1, source_target_pairs={{0,3},{1,0},{2,1},{3,2},{4,7},{5,4},{6,5},{7,6},{8,11},{9,8},{10,9... | collective-permute-start | bytes 1179656 | tf_op jit(solution)/shard_map/ppermute | solution.py:90
  217.6 0.8 copy-start.6
Sparse Core Ops, SparseCore 0:
  63.6 39.5 all-gather.2
  136.6 48.6 all-gather.4

commit v2 on v1

--- a/solution.py
+++ b/solution.py
@@ -14,7 +14,7 @@
 MODE = ("offload", "ring", "offload", "ring")
 EPS = 1e-05
 OWN = ("section", "seq")
-KERNEL_VMEM = 62 << 20
+KERNEL_VMEM = 127 << 19
 
 
 def scatter_rows(position, pieces, offset, rows, cells):
@@ -162,6 +162,76 @@
         ),
         name="norm_and_project",
     )(here, gain.reshape(1, depth), key_matrix, value_matrix, *[x for _, _, x in parts])
+
+
+def project_parts(parts, scale, gain, key_matrix, value_matrix, sums=None):
+    rows = scale.shape[0]
+    width = parts[0][2].shape[1]
+    depth, columns = key_matrix.shape
+    size = depth // width
+    tile = 256
+    block = 16
+    here = lax.axis_index("tp").astype(jnp.int32).reshape(1)
+    steps = list(dict.fromkeys(step for step, _, _ in parts))
+    n, m = len(parts), len(steps)
+
+    def body(here_ref, scale_ref, *refs):
+        gain_refs, key_refs, value_refs = refs[:m], refs[m : 2 * m], refs[2 * m : 3 * m]
+        part_refs, refs = refs[3 * m : 3 * m + n], refs[3 * m + n :]
+        sum_refs, (key_out, value_out, encoded) = refs[:-3], refs[-3:]
+
+        @pl.when(pl.program_id(0) == 0)
+        def _():
+            for (step, start, _), ref in zip(parts, part_refs):
+                p = steps.index(step)
+
+                @pl.loop(0, ref.shape[0] // block, unroll=2)
+                def _(b):
+                    at = pl.multiple_of(b * block, block)
+                    x = ref[pl.ds(at, block), :].astype(jnp.float32)
+                    x = x * scale_ref[pl.ds(pl.multiple_of(start + at, block), block), :1] * gain_refs[p][...]
+                    encoded[p, pl.ds(pl.multiple_of(start + at, block), block), :] = x.astype(jnp.bfloat16)
+
+        key_sum = sum(jnp.dot(encoded[p], key_refs[p][...], preferred_element_type=jnp.float32) for p in range(m))
+        value_sum = sum(jnp.dot(encoded[p], value_refs[p][...], preferred_element_type=jnp.float32) for p in range(m))
+        if sum_refs:
+            key_sum, value_sum = sum_refs[0][...] + key_sum, sum_refs[1][...] + value_sum
+        key_out[...] = key_sum.astype(key_out.dtype)
+        value_out[...] = value_sum.astype(value_out.dtype)
+
+    sums = list(sums) if sums is not None else []
+    column = pl.BlockSpec((rows, tile), lambda i, here: (0, i))
+    matrix = [pl.BlockSpec((width, tile), lambda i, here, s=s: ((here[0] + s) % size, i)) for s in steps]
+    out = jax.ShapeDtypeStruct((rows, columns), jnp.bfloat16 if sums else jnp.float32)
+    return pl.pallas_call(
+        body,
+        grid_spec=pltpu.PrefetchScalarGridSpec(
+            num_scalar_prefetch=1,
+            grid=(columns // tile,),
+            in_specs=[pl.BlockSpec(scale.shape, lambda i, here: (0, 0))]
+            + [pl.BlockSpec((1, width), lambda i, here, s=s: (0, (here[0] + s) % size)) for s in steps]
+            + matrix
+            + matrix
+            + [pl.BlockSpec(x.shape, lambda i, here: (0, 0)) for _, _, x in parts]
+            + [column] * len(sums),
+            out_specs=(column, column),
+            scratch_shapes=[pltpu.VMEM((m, rows, width), jnp.bfloat16)],
+        ),
+        out_shape=(out, out),
+        compiler_params=pltpu.CompilerParams(vmem_limit_bytes=KERNEL_VMEM),
+        cost_estimate=pl.CostEstimate(
+            flops=4 * rows * m * width * columns, bytes_accessed=4 * m * width * columns, transcendentals=0
+        ),
+        name="project_parts",
+    )(
+        here,
+        scale,
+        *[gain.reshape(1, depth)] * m,
+        *[key_matrix] * m,
+        *[value_matrix] * m,
+        *[x for _, _, x in parts],
+        *sums,
+    )
 
 
 def attend(queries, keys, values, counts):
@@ -274,8 +344,9 @@
         if j == 0:
             arrived = after(arrived, *picked[1:])
         if j >= 3:
-            finish(j - 3)
-            arrived = after(arrived, done[j - 3][0])
+            finish(0)
+            finish(1)
+            arrived = after(arrived, done[0][0], done[1][0])
         if j - 1 in halves:
             arrived = after(arrived, *halves[j - 1])
         own = place(j, arrived)
@@ -288,11 +359,21 @@
         halves[j] = up[:half], down[half:]
         far = send(halves[j][0], 1), send(halves[j][1], size - 1)
         parts.append([(0, 0, own), (size - 1, 0, up), (1, 0, down), (2, 0, far[0]), (2, half, far[1])])
-    parts[-2][-1] = parts[-2][-1][:2] + (after(parts[-2][-1][2], *halves[count - 1]),)
-    parts[-3][-1] = parts[-3][-1][:2] + (after(parts[-3][-1][2], parts[-1][0][2]),)
-    for j in range(count):
+    last = count - 1
+    own = parts[last][0][2]
+    squares = jnp.sum(jnp.square(own.astype(jnp.float32)), -1)
+    squares = squares + send(squares, 1) + send(squares, 2) + send(squares, 3)
+    scale = lax.rsqrt(squares * (1.0 / (size * width_part)) + EPS)
+    scale = jnp.broadcast_to(scale[:, None], (scale.shape[0], HD))
+    for j in range(last):
         if j not in done:
+            parts[j][-1] = parts[j][-1][:2] + (after(parts[j][-1][2], own),)
             finish(j)
+    halves[last] = lax.optimization_barrier((*halves[last], *[done[j][0] for j in range(last)]))[:2]
+    matrices = norm_gain, key_weight[0], value_weight[0]
+    parts[last][3:] = [(2, 0, send(halves[last][0], 1)), (2, own.shape[0] // 2, send(halves[last][1], size - 1))]
+    sums = project_parts(parts[last][:3], after(scale, *halves[last]), *matrices)
+    done[last] = project_parts(parts[last][3:], scale, *matrices, sums=sums)
     keys = [done[j][0] for j in range(count)]
     values = [done[j][1] for j in range(count)]
     keys = [shape_rows(x) for x in keys]

time: 247 us -> 275 us (1.11)
  waiting for transfers between devices: 82.4 us -> 95.5 us
  Pallas kernels: 85.9 us -> 92.5 us
  starting transfers between devices: 41.3 us -> 45.6 us
  local copies, waits for them, and re-layouts: 5.74 us -> 8.98 us
    ppermute x8 -> x11, waiting for transfers between devices: 23.7 us -> 48.1 us  [send(): return lax.ppermute(x, 'tp', [(i, (i + step) % size) for i in range(size)])]
    pallas_call x0 -> x2, Pallas kernels: none -> 20.7 us  [project_parts(): pl.pallas_call(body, grid_spec=pltpu.PrefetchScalarGridSpec(num_scalar_pr...]
    pallas_call x4 -> x3, Pallas kernels: 56.4 us -> 42.3 us  [project(): pl.pallas_call(body, grid=(columns // tile,), out_shape=(out, out), in_sp...]
    all_to_all x4, waiting for transfers between devices: 58.6 us -> 47.4 us  [per_device(): lax.all_to_all(ready, OWN, split_axis=0, concat_axis=0, tiled=True)]
    ppermute x8 -> x11, starting transfers between devices: 15.9 us -> 19.6 us  [send(): return lax.ppermute(x, 'tp', [(i, (i + step) % size) for i in range(size)])]
  transfers between devices with their start and end apart: 14 -> 17, of which waited for: 6 -> 7; matrix products, arithmetic and copies ran while one was open for 1% -> 1% of each run, Pallas kernels for 24% -> 27%
where the time goes in v2:
time: 275 us; the launch traced here: 274 us
  waiting for transfers between devices  95.5 us (35%)
  Pallas kernels  92.5 us (34%)
  starting transfers between devices  45.6 us (17%)
  blocking collectives  13.6 us (5%)
  between operations  13.6 us (5%)
  local copies, waits for them, and re-layouts  8.98 us (3%)
  other arithmetic  4.4 us (2%)
    ppermute x11, waiting for transfers between devices, send(): return lax.ppermute(x, 'tp', [(i, (i + step) % size) for i in range(size)])  48.1 us
    all_to_all x4, waiting for transfers between devices, per_device(): lax.all_to_all(ready, OWN, split_axis=0, concat_axis=0, tiled=True)  47.4 us
    pallas_call x3, Pallas kernels, project(): pl.pallas_call(body, grid=(columns // tile,), out_shape=(out, out), in_sp...  42.3 us
    all_to_all x4, starting transfers between devices, per_device(): lax.all_to_all(ready, OWN, split_axis=0, concat_axis=0, tiled=True)  25.9 us
    pallas_call x2, Pallas kernels, project_parts(): pl.pallas_call(body, grid_spec=pltpu.PrefetchScalarGridSpec(num_scalar_pr...  20.7 us
    ppermute x11, starting transfers between devices, send(): return lax.ppermute(x, 'tp', [(i, (i + step) % size) for i in range(size)])  19.6 us
    all_to_all x1, blocking collectives, per_device(): lax.all_to_all(request.reshape(owners, capacity), OWN, split_axis=0, conc...  13.6 us
    pallas_call x4, Pallas kernels, scatter_rows(): pl.pallas_call(body, out_shape=jax.ShapeDtypeStruct((cells, rows, width),...  11.8 us
  transfers between devices with their start and end apart: 17, of which 7 were waited for; matrix products, arithmetic and copies ran while one was open for 1% of the time, Pallas kernels for 27%

profile of v2, /device:TPU:2, one launch (start us, length us, event | category | flops | bytes accessed | tf_op | source)
XLA Modules:
  0.0 274.1 jit_solution(11986968481956870506)
XLA Ops:
  8.3 13.6 %all_to_all.26 = s32[32,1,2]{2,1,0:T(1,128)S(1)} all-to-all(s32[32,1,2]{2,1,0:T(1,128)S(1)} %bitcast.71), channel_id=1, replica_groups=mesh['section'=4,'seq'=8,'tp'=4] {'section','seq'}, dimensions={0} | all-to-all | bytes 512 | tf_op jit(solution)/shard_map/all_to_all | solution.py:311
  23.8 2.9 %pick_rows.4 = bf16[64,16,1024]{2,1,0:T(8,128)(2,1)} custom-call(s32[24]{0:T(128)} %select_reduce_fusion.position_ref, bf16[24,64,1024]{2,1,0:T(8,128)(2,1)} %bitcast.40), custom_call_target="tpu_custom_call" | custom-call | bytes 1572864 | tf_op jit(solution)/shard_map/pick_rows/pallas_call | solution.py:36
  26.8 5.8 %all-to-all-start.1 = ((bf16[32,2,16,1024]{3,2,1,0:T(8,128)(2,1)}), bf16[32,2,16,1024]{3,2,1,0:T(8,128)(2,1)}, u32[]{:S(2)}, u32[]{:S(2)}) async-start(bf16[32,2,16,1024]{3,2,1,0:T(8,128)(2,1)} %bitcast.47), calls=%async_computation.1 | async-start | bytes 4194304 | tf_op jit(solution)/shard_map/all_to_all | solution.py:343
  32.7 2.9 %pick_rows.5 = bf16[64,16,1024]{2,1,0:T(8,128)(2,1)} custom-call(s32[24]{0:T(128)} %select_reduce_fusion.position_ref, bf16[24,64,1024]{2,1,0:T(8,128)(2,1)} %bitcast.41), custom_call_target="tpu_custom_call" | custom-call | bytes 1572864 | tf_op jit(solution)/shard_map/pick_rows/pallas_call | solution.py:36
  35.6 3.0 %pick_rows.6 = bf16[64,16,1024]{2,1,0:T(8,128)(2,1)} custom-call(s32[24]{0:T(128)} %select_reduce_fusion.position_ref, bf16[24,64,1024]{2,1,0:T(8,128)(2,1)} %bitcast.42), custom_call_target="tpu_custom_call" | custom-call | bytes 1572864 | tf_op jit(solution)/shard_map/pick_rows/pallas_call | solution.py:36
  38.6 2.9 %pick_rows.7 = bf16[64,16,1024]{2,1,0:T(8,128)(2,1)} custom-call(s32[24]{0:T(128)} %select_reduce_fusion.position_ref, bf16[24,64,1024]{2,1,0:T(8,128)(2,1)} %bitcast.43), custom_call_target="tpu_custom_call" | custom-call | bytes 1572864 | tf_op jit(solution)/shard_map/pick_rows/pallas_call | solution.py:36
  41.5 19.1 %all-to-all-done.1 = bf16[32,2,16,1024]{3,2,1,0:T(8,128)(2,1)} async-done(((bf16[32,2,16,1024]{3,2,1,0:T(8,128)(2,1)}), bf16[32,2,16,1024]{3,2,1,0:T(8,128)(2,1)}, u32[]{:S(2)}, u32[]{:S(2)}) %all-to-all-start.1) | async-done | bytes 2097184 | tf_op jit(solution)/shard_map/all_to_all | solution.py:343
  60.6 2.8 %place_rows.4 = bf16[24,16,1024]{2,1,0:T(8,128)(2,1)} custom-call(s32[24]{0:T(128)} %copy-done.5, bf16[64,16,1024]{2,1,0:T(8,128)(2,1)} %bitcast.10.cells_ref), custom_call_target="tpu_custom_call" | custom-call | bytes 1572864 | tf_op jit(solution)/shard_map/place_rows/pallas_call | solution.py:68
  63.5 6.0 %all-to-all-start.2 = ((bf16[32,2,16,1024]{3,2,1,0:T(8,128)(2,1)}), bf16[32,2,16,1024]{3,2,1,0:T(8,128)(2,1)S(1)}, u32[]{:S(2)}, u32[]{:S(2)}) async-start(bf16[32,2,16,1024]{3,2,1,0:T(8,128)(2,1)} %bitcast.45), calls=%async_computation.2 | async-start | bytes 4194304 | tf_op jit(solution)/shard_map/all_to_all | solution.py:343
  69.6 28.0 %all-to-all-done.2 = bf16[32,2,16,1024]{3,2,1,0:T(8,128)(2,1)S(1)} async-done(((bf16[32,2,16,1024]{3,2,1,0:T(8,128)(2,1)}), bf16[32,2,16,1024]{3,2,1,0:T(8,128)(2,1)S(1)}, u32[]{:S(2)}, u32[]{:S(2)}) %all-to-all-start.2) | async-done | bytes 2097184 | tf_op jit(solution)/shard_map/all_to_all | solution.py:343
  98.9 6.7 %all-to-all-start.3 = ((bf16[32,2,16,1024]{3,2,1,0:T(8,128)(2,1)}), bf16[32,2,16,1024]{3,2,1,0:T(8,128)(2,1)}, u32[]{:S(2)}, u32[]{:S(2)}) async-start(bf16[32,2,16,1024]{3,2,1,0:T(8,128)(2,1)} %bitcast.8), calls=%async_computation.3 | async-start | bytes 4194304 | tf_op jit(solution)/shard_map/all_to_all | solution.py:343
  105.6 2.9 %place_rows.5 = bf16[24,16,1024]{2,1,0:T(8,128)(2,1)} custom-call(s32[24]{0:T(128)} %copy-done.5, bf16[64,16,1024]{2,1,0:T(8,128)(2,1)} %bitcast.46), custom_call_target="tpu_custom_call" | custom-call | bytes 1572864 | tf_op jit(solution)/shard_map/place_rows/pallas_call | solution.py:68
  108.6 2.0 collective-permute-start
  110.5 2.2 collective-permute-start.1
  112.7 18.0 %collective-permute-done.refs_1_ = bf16[384,1024]{1,0:T(8,128)(2,1)S(1)} collective-permute-done((bf16[384,1024]{1,0:T(8,128)(2,1)}, bf16[384,1024]{1,0:T(8,128)(2,1)S(1)}, u32[]{:S(2)}, u32[]{:S(2)}) %collective-permute-start) | collective-permute-done | bytes 786464 | tf_op jit(solution)/shard_map/ppermute | solution.py:90
  133.6 2.9 %place_rows.6 = bf16[24,16,1024]{2,1,0:T(8,128)(2,1)} custom-call(s32[24]{0:T(128)} %copy-done.5, bf16[64,16,1024]{2,1,0:T(8,128)(2,1)} %bitcast.16.cells_ref), custom_call_target="tpu_custom_call" | custom-call | bytes 1572864 | tf_op jit(solution)/shard_map/place_rows/pallas_call | solution.py:68
  136.5 7.4 %all-to-all-start.4 = ((bf16[32,2,16,1024]{3,2,1,0:T(8,128)(2,1)}), bf16[32,2,16,1024]{3,2,1,0:T(8,128)(2,1)}, u32[]{:S(2)}, u32[]{:S(2)}) async-start(bf16[32,2,16,1024]{3,2,1,0:T(8,128)(2,1)} %bitcast.44), calls=%async_computation.4 | async-start | bytes 4194304 | tf_op jit(solution)/shard_map/all_to_all | solution.py:343
  145.4 2.2 collective-permute-start.3
  147.6 15.8 %collective-permute-done.2.refs_3_ = bf16[192,1024]{1,0:T(8,128)(2,1)S(1)} collective-permute-done((bf16[192,1024]{1,0:T(8,128)(2,1)S(1)}, bf16[192,1024]{1,0:T(8,128)(2,1)S(1)}, u32[]{:S(2)}, u32[]{:S(2)}) %collective-permute-start.2) | collective-permute-done | bytes 393248 | tf_op jit(solution)/shard_map/ppermute | solution.py:90
  165.6 14.1 %norm_and_project.4 = (bf16[384,1024]{1,0:T(8,128)(2,1)}, bf16[384,1024]{1,0:T(8,128)(2,1)}) custom-call(s32[1]{0:T(128)} %bitcast.here_ref, f32[1,4096]{1,0:T(1,128)} %bitcast.64, bf16[4096,1024]{1,0:T(8,128)(2,1)} %bitcast.26, bf16[4096,1024]{1,0:T(8,128)(2,1)} %bitcast.33, bf16[384,1024]{1,0:T(8,128)(2,1)} %bitcast.55, bf16[384,1024]{1,0:T(8,128)(2,1)} %copy-done.3, ...), custom_call_target="tpu_custom_call" | custom-call | flops 6442450944 | bytes 19922944 | tf_op jit(solution)/shard_map/norm_and_project/pallas_call | solution.py:146
  179.7 14.1 %norm_and_project.3 = (bf16[384,1024]{1,0:T(8,128)(2,1)}, bf16[384,1024]{1,0:T(8,128)(2,1)}) custom-call(s32[1]{0:T(128)} %bitcast.here_ref, f32[1,4096]{1,0:T(1,128)} %bitcast.65, bf16[4096,1024]{1,0:T(8,128)(2,1)} %bitcast.27, bf16[4096,1024]{1,0:T(8,128)(2,1)} %bitcast.34, bf16[4,384,1024]{2,1,0:T(8,128)(2,1)} %all-gather.3.cloned.1.call-done.refs_0_), custom_call_target="tpu_custom_call" | custom-call | flops 6442450944 | bytes 19922944 | tf_op jit(solution)/shard_map/norm_and_project/pallas_call | solution.py:146
  193.8 2.8 %place_rows.7 = bf16[24,16,1024]{2,1,0:T(8,128)(2,1)} custom-call(s32[24]{0:T(128)} %copy-done.5, bf16[64,16,1024]{2,1,0:T(8,128)(2,1)} %bitcast.18.cells_ref), custom_call_target="tpu_custom_call" | custom-call | bytes 1572864 | tf_op jit(solution)/shard_map/place_rows/pallas_call | solution.py:68
  199.4 2.5 collective-permute-start.6
  201.9 1.6 collective-permute-start.5
  204.7 1.9 collective-permute-start.8
  206.7 12.8 %collective-permute-done.5 = f32[384]{0:T(512)S(1)} collective-permute-done((f32[384]{0:T(512)S(1)}, f32[384]{0:T(512)S(1)}, u32[]{:S(2)}, u32[]{:S(2)}) %collective-permute-start.5) | collective-permute-done | bytes 1568 | tf_op jit(solution)/shard_map/ppermute | solution.py:90
  220.5 14.1 %norm_and_project.5 = (bf16[384,1024]{1,0:T(8,128)(2,1)}, bf16[384,1024]{1,0:T(8,128)(2,1)}) custom-call(s32[1]{0:T(128)} %bitcast.here_ref, f32[1,4096]{1,0:T(1,128)} %bitcast.66, bf16[4096,1024]{1,0:T(8,128)(2,1)} %bitcast.28, bf16[4096,1024]{1,0:T(8,128)(2,1)} %bitcast.35, bf16[4,384,1024]{2,1,0:T(8,128)(2,1)} %all-gather.5.cloned.1.call-done.refs_0_), custom_call_target="tpu_custom_call" | custom-call | flops 6442450944 | bytes 19922944 | tf_op jit(solution)/shard_map/norm_and_project/pallas_call | solution.py:146
  234.5 1.8 slice.19
  236.3 3.2 %collective-permute-start.10 = (bf16[192,1024]{1,0:T(8,128)(2,1)}, bf16[192,1024]{1,0:T(8,128)(2,1)}, u32[]{:S(2)}, u32[]{:S(2)}) collective-permute-start(bf16[192,1024]{1,0:T(8,128)(2,1)} %slice.19), channel_id=1, source_target_pairs={{0,3},{1,0},{2,1},{3,2},{4,7},{5,4},{6,5},{7,6},{8,11},{9,8},{10,9... | collective-permute-start | bytes 1179656 | tf_op jit(solution)/shard_map/ppermute | solution.py:90
  240.3 13.4 %project_parts.2 = (f32[384,1024]{1,0:T(8,128)}, f32[384,1024]{1,0:T(8,128)}) custom-call(s32[1]{0:T(128)} %bitcast.here_ref, f32[384,128]{1,0:T(8,128)} %broadcast_in_dim.43.scale_ref, f32[1,4096]{1,0:T(1,128)} %bitcast.67, f32[1,4096]{1,0:T(1,128)} %bitcast.68, f32[1,4096]{1,0:T(1,128)} %bitcast.69, bf16[4096,1024]{1,0:T(8,128)(2,1)} %bitcast.29, ...), custom_call_target="tpu_custom_call" | custom-call | flops 4831838208 | bytes 12582912 | tf_op jit(solution)/shard_map/project_parts/pallas_call | solution.py:206
  253.7 7.4 %project_parts.3 = (bf16[384,1024]{1,0:T(8,128)(2,1)}, bf16[384,1024]{1,0:T(8,128)(2,1)}) custom-call(s32[1]{0:T(128)} %bitcast.here_ref, f32[384,128]{1,0:T(8,128)} %broadcast_in_dim.43.scale_ref, f32[1,4096]{1,0:T(1,128)} %bitcast.70, bf16[4096,1024]{1,0:T(8,128)(2,1)} %bitcast.32, bf16[4096,1024]{1,0:T(8,128)(2,1)} %bitcast.39, ...), custom_call_target="tpu_custom_call" | custom-call | flops 1610612736 | bytes 4194304 | tf_op jit(solution)/shard_map/project_parts/pallas_call | solution.py:206
  261.1 6.2 %attention.1 = bf16[384,1024]{1,0:T(8,128)(2,1)} custom-call(s32[6]{0:T(128)} %count_ref.1, bf16[384,1024]{1,0:T(8,128)(2,1)} %query_ref.1, bf16[6,64,1024]{2,1,0:T(8,128)(2,1)} %bitcast.58, bf16[6,64,1024]{2,1,0:T(8,128)(2,1)} %bitcast.56, bf16[6,64,1024]{2,1,0:T(8,128)(2,1)} %bitcast.60, bf16[6,64,1024]{2,1,0:T(8,128)(2,1)} %bitcast.62, ...), custom_call_target="tpu_custom_call" | custom-call | flops 402653184 | bytes 7864320 | tf_op jit(solution)/shard_map/attention/pallas_call | solution.py:280
  (53 shorter events, 17.5 us)
Async XLA Ops:
  8.1 18.7 %copy-start.5 = (s32[24]{0:T(128)}, s32[24]{0:T(128)S(1)}, u32[]{:S(2)}) copy-start(s32[24]{0:T(128)S(1)} %multiply_add_fusion.position_ref) | copy-start | bytes 292
  26.8 33.8 %all-to-all-start.1 = ((bf16[32,2,16,1024]{3,2,1,0:T(8,128)(2,1)}), bf16[32,2,16,1024]{3,2,1,0:T(8,128)(2,1)}, u32[]{:S(2)}, u32[]{:S(2)}) async-start(bf16[32,2,16,1024]{3,2,1,0:T(8,128)(2,1)} %bitcast.47), calls=%async_computation.1 | async-start | bytes 4194304 | tf_op jit(solution)/shard_map/all_to_all | solution.py:343
  32.6 147.1 %all-gather.3.cloned.1.call-start = ((), (), s32[]{:S(2)}) async-start(), calls=%async_computation.5 | async-start | bytes 3932160 | tf_op jit(solution)/shard_map/all_gather | solution.py:354
  63.5 34.0 %all-to-all-start.2 = ((bf16[32,2,16,1024]{3,2,1,0:T(8,128)(2,1)}), bf16[32,2,16,1024]{3,2,1,0:T(8,128)(2,1)S(1)}, u32[]{:S(2)}, u32[]{:S(2)}) async-start(bf16[32,2,16,1024]{3,2,1,0:T(8,128)(2,1)} %bitcast.45), calls=%async_computation.2 | async-start | bytes 4194304 | tf_op jit(solution)/shard_map/all_to_all | solution.py:343
  97.5 1.4 copy-start
  98.9 34.7 %all-to-all-start.3 = ((bf16[32,2,16,1024]{3,2,1,0:T(8,128)(2,1)}), bf16[32,2,16,1024]{3,2,1,0:T(8,128)(2,1)}, u32[]{:S(2)}, u32[]{:S(2)}) async-start(bf16[32,2,16,1024]{3,2,1,0:T(8,128)(2,1)} %bitcast.8), calls=%async_computation.3 | async-start | bytes 4194304 | tf_op jit(solution)/shard_map/all_to_all | solution.py:343
  105.6 113.9 %all-gather.5.cloned.1.call-start = ((), (), s32[]{:S(2)}) async-start(), calls=%async_computation.6 | async-start | bytes 3932160 | tf_op jit(solution)/shard_map/all_gather | solution.py:354
  108.6 22.2 %collective-permute-start = (bf16[384,1024]{1,0:T(8,128)(2,1)}, bf16[384,1024]{1,0:T(8,128)(2,1)S(1)}, u32[]{:S(2)}, u32[]{:S(2)}) collective-permute-start(bf16[384,1024]{1,0:T(8,128)(2,1)} %bitcast.53), channel_id=1, source_target_pairs={{0,1},{1,2},{2,3},{3,0},{4,5},{5,6},{6,7},{7,4},{8,9},{9,10},{10,1... | collective-permute-start | bytes 2359304 | tf_op jit(solution)/shard_map/ppermute | solution.py:90
  110.5 21.1 %collective-permute-start.1 = (bf16[384,1024]{1,0:T(8,128)(2,1)}, bf16[384,1024]{1,0:T(8,128)(2,1)S(1)}, u32[]{:S(2)}, u32[]{:S(2)}) collective-permute-start(bf16[384,1024]{1,0:T(8,128)(2,1)} %bitcast.54), channel_id=1, source_target_pairs={{0,3},{1,0},{2,1},{3,2},{4,7},{5,4},{6,5},{7,6},{8,11},{9,8},{10,9... | collective-permute-start | bytes 2359304 | tf_op jit(solution)/shard_map/ppermute | solution.py:90
  130.7 0.9 copy-start.3
  131.6 0.9 copy-start.4
  136.5 8.9 %copy-start.2 = (bf16[192,1024]{1,0:T(8,128)(2,1)S(1)}, bf16[192,1024]{1,0:T(8,128)(2,1)}, u32[]{:S(2)}) copy-start(bf16[192,1024]{1,0:T(8,128)(2,1)} %slice.17) | copy-start | bytes 1179652
  136.5 57.3 %all-to-all-start.4 = ((bf16[32,2,16,1024]{3,2,1,0:T(8,128)(2,1)}), bf16[32,2,16,1024]{3,2,1,0:T(8,128)(2,1)}, u32[]{:S(2)}, u32[]{:S(2)}) async-start(bf16[32,2,16,1024]{3,2,1,0:T(8,128)(2,1)} %bitcast.44), calls=%async_computation.4 | async-start | bytes 4194304 | tf_op jit(solution)/shard_map/all_to_all | solution.py:343
  143.9 19.5 %collective-permute-start.2 = (bf16[192,1024]{1,0:T(8,128)(2,1)S(1)}, bf16[192,1024]{1,0:T(8,128)(2,1)S(1)}, u32[]{:S(2)}, u32[]{:S(2)}) collective-permute-start(bf16[192,1024]{1,0:T(8,128)(2,1)S(1)} %slice.16), channel_id=1, source_target_pairs={{0,1},{1,2},{2,3},{3,0},{4,5},{5,6},{6,7},{7,4},{8,9},{9,10},{10,1... | collective-permute-start | bytes 1179656 | tf_op jit(solution)/shard_map/ppermute | solution.py:90
  145.4 19.5 %collective-permute-start.3 = (bf16[192,1024]{1,0:T(8,128)(2,1)S(1)}, bf16[192,1024]{1,0:T(8,128)(2,1)S(1)}, u32[]{:S(2)}, u32[]{:S(2)}) collective-permute-start(bf16[192,1024]{1,0:T(8,128)(2,1)S(1)} %copy-done.2), channel_id=1, source_target_pairs={{0,3},{1,0},{2,1},{3,2},{4,7},{5,4},{6,5},{7,6},{8,11},{9,8},{10,9... | collective-permute-start | bytes 1179656 | tf_op jit(solution)/shard_map/ppermute | solution.py:90
  163.4 1.4 copy-start.6
  164.9 0.8 copy-start.7
  196.7 22.8 %collective-permute-start.7 = (bf16[384,1024]{1,0:T(8,128)(2,1)}, bf16[384,1024]{1,0:T(8,128)(2,1)S(1)}, u32[]{:S(2)}, u32[]{:S(2)}) collective-permute-start(bf16[384,1024]{1,0:T(8,128)(2,1)} %bitcast.48), channel_id=1, source_target_pairs={{0,1},{1,2},{2,3},{3,0},{4,5},{5,6},{6,7},{7,4},{8,9},{9,10},{10,1... | collective-permute-start | bytes 2359304 | tf_op jit(solution)/shard_map/ppermute | solution.py:90
  199.4 7.3 %collective-permute-start.6 = (f32[384]{0:T(512)S(1)}, f32[384]{0:T(512)S(1)}, u32[]{:S(2)}, u32[]{:S(2)}) collective-permute-start(f32[384]{0:T(512)S(1)} %reduce_sum.32), channel_id=1, source_target_pairs={{0,3},{1,0},{2,1},{3,2},{4,7},{5,4},{6,5},{7,6},{8,11},{9,8},{10,9... | collective-permute-start | bytes 4616 | tf_op jit(solution)/shard_map/ppermute | solution.py:90
  201.9 17.6 %collective-permute-start.5 = (f32[384]{0:T(512)S(1)}, f32[384]{0:T(512)S(1)}, u32[]{:S(2)}, u32[]{:S(2)}) collective-permute-start(f32[384]{0:T(512)S(1)} %reduce_sum.32), channel_id=1, source_target_pairs={{0,2},{1,3},{2,0},{3,1},{4,6},{5,7},{6,4},{7,5},{8,10},{9,11},{10,... | collective-permute-start | bytes 4616 | tf_op jit(solution)/shard_map/ppermute | solution.py:90
  203.4 16.0 %collective-permute-start.4 = (f32[384]{0:T(512)S(1)}, f32[384]{0:T(512)S(1)}, u32[]{:S(2)}, u32[]{:S(2)}) collective-permute-start(f32[384]{0:T(512)S(1)} %reduce_sum.32), channel_id=1, source_target_pairs={{0,1},{1,2},{2,3},{3,0},{4,5},{5,6},{6,7},{7,4},{8,9},{9,10},{10,1... | collective-permute-start | bytes 4616 | tf_op jit(solution)/shard_map/ppermute | solution.py:90
  204.7 29.8 %collective-permute-start.8 = (bf16[384,1024]{1,0:T(8,128)(2,1)}, bf16[384,1024]{1,0:T(8,128)(2,1)}, u32[]{:S(2)}, u32[]{:S(2)}) collective-permute-start(bf16[384,1024]{1,0:T(8,128)(2,1)} %bitcast.49), channel_id=1, source_target_pairs={{0,3},{1,0},{2,1},{3,2},{4,7},{5,4},{6,5},{7,6},{8,11},{9,8},{10,9... | collective-permute-start | bytes 2359304 | tf_op jit(solution)/shard_map/ppermute | solution.py:90
  219.5 0.9 copy-start.1
  236.3 17.4 %collective-permute-start.9 = (bf16[192,1024]{1,0:T(8,128)(2,1)S(1)}, bf16[192,1024]{1,0:T(8,128)(2,1)}, u32[]{:S(2)}, u32[]{:S(2)}) collective-permute-start(bf16[192,1024]{1,0:T(8,128)(2,1)S(1)} %slice.18), channel_id=1, source_target_pairs={{0,1},{1,2},{2,3},{3,0},{4,5},{5,6},{6,7},{7,4},{8,9},{9,10},{10,1... | collective-permute-start | bytes 1179656 | tf_op jit(solution)/shard_map/ppermute | solution.py:90
  236.3 17.4 %collective-permute-start.10 = (bf16[192,1024]{1,0:T(8,128)(2,1)}, bf16[192,1024]{1,0:T(8,128)(2,1)}, u32[]{:S(2)}, u32[]{:S(2)}) collective-permute-start(bf16[192,1024]{1,0:T(8,128)(2,1)} %slice.19), channel_id=1, source_target_pairs={{0,3},{1,0},{2,1},{3,2},{4,7},{5,4},{6,5},{7,6},{8,11},{9,8},{10,9... | collective-permute-start | bytes 1179656 | tf_op jit(solution)/shard_map/ppermute | solution.py:90
Sparse Core Ops, SparseCore 0:
  63.6 39.5 all-gather.2
  136.6 45.9 all-gather.4

commit v3 on v1

--- a/solution.py
+++ b/solution.py
@@ -10,11 +10,11 @@
 HD = 128
 PIECE = 64
 NBR = 2
-CHUNKS = (16, 16, 16, 16)
-MODE = ("offload", "ring", "offload", "ring")
+CHUNKS = (32, 16, 16)
+MODE = ("offload", "ring", "ring")
 EPS = 1e-05
 OWN = ("section", "seq")
-KERNEL_VMEM = 62 << 20
+KERNEL_VMEM = 127 << 19
 
 
 def scatter_rows(position, pieces, offset, rows, cells):
@@ -284,12 +284,15 @@
             parts.append([(0, 0, own), (None, 0, full)])
             continue
         up, down = send(own, 1), send(own, size - 1)
+        if j == count - 1:
+            parts[0][-1] = parts[0][-1][:2] + (after(parts[0][-1][2], own),)
+            finish(0)
+            up, down = lax.optimization_barrier((up, down, done[0][0]))[:2]
         half = own.shape[0] // 2
         halves[j] = up[:half], down[half:]
         far = send(halves[j][0], 1), send(halves[j][1], size - 1)
         parts.append([(0, 0, own), (size - 1, 0, up), (1, 0, down), (2, 0, far[0]), (2, half, far[1])])
     parts[-2][-1] = parts[-2][-1][:2] + (after(parts[-2][-1][2], *halves[count - 1]),)
-    parts[-3][-1] = parts[-3][-1][:2] + (after(parts[-3][-1][2], parts[-1][0][2]),)
     for j in range(count):
         if j not in done:
             finish(j)

time: 247 us -> 254 us (1.028)
  waiting for transfers between devices: 82.4 us -> 107 us
  Pallas kernels: 85.9 us -> 75.9 us
  starting transfers between devices: 41.3 us -> 32 us
    all_to_all x4 -> x3, waiting for transfers between devices: 58.6 us -> 73.5 us  [per_device(): lax.all_to_all(ready, OWN, split_axis=0, concat_axis=0, tiled=True)]
    ppermute x8, waiting for transfers between devices: 23.7 us -> 33.1 us  [send(): return lax.ppermute(x, 'tp', [(i, (i + step) % size) for i in range(size)])]
    all_to_all x4 -> x3, starting transfers between devices: 25.3 us -> 18.7 us  [per_device(): lax.all_to_all(ready, OWN, split_axis=0, concat_axis=0, tiled=True)]
    pallas_call x4 -> x3, Pallas kernels: 56.4 us -> 51.3 us  [project(): pl.pallas_call(body, grid=(columns // tile,), out_shape=(out, out), in_sp...]
    slice x4, local copies, waits for them, and re-layouts: 1.27 us -> 4.33 us  [per_device(): halves[j] = (up[:half], down[half:])]
    ppermute x8, starting transfers between devices: 15.9 us -> 13.3 us  [send(): return lax.ppermute(x, 'tp', [(i, (i + step) % size) for i in range(size)])]
    pallas_call x4 -> x3, Pallas kernels: 11.8 us -> 9.28 us  [scatter_rows(): pl.pallas_call(body, out_shape=jax.ShapeDtypeStruct((cells, rows, width),...]
    pallas_call x4 -> x3, Pallas kernels: 11.5 us -> 9.16 us  [gather_rows(): pl.pallas_call(body, out_shape=jax.ShapeDtypeStruct((count, rows, width),...]
  transfers between devices with their start and end apart: 14 -> 12, of which waited for: 6 -> 3; matrix products, arithmetic and copies ran while one was open for 1% -> 2% of each run, Pallas kernels for 24% -> 19%
where the time goes in v3:
time: 254 us; the launch traced here: 253 us
  waiting for transfers between devices  107 us (42%)
  Pallas kernels  75.9 us (30%)
  starting transfers between devices  32 us (13%)
  blocking collectives  13.6 us (5%)
  between operations  13.6 us (5%)
  local copies, waits for them, and re-layouts  8.06 us (3%)
  other arithmetic  3.01 us (1%)
    all_to_all x3, waiting for transfers between devices, per_device(): lax.all_to_all(ready, OWN, split_axis=0, concat_axis=0, tiled=True)  73.5 us
    pallas_call x3, Pallas kernels, project(): pl.pallas_call(body, grid=(columns // tile,), out_shape=(out, out), in_sp...  51.3 us
    ppermute x8, waiting for transfers between devices, send(): return lax.ppermute(x, 'tp', [(i, (i + step) % size) for i in range(size)])  33.1 us
    all_to_all x3, starting transfers between devices, per_device(): lax.all_to_all(ready, OWN, split_axis=0, concat_axis=0, tiled=True)  18.7 us
    all_to_all x1, blocking collectives, per_device(): lax.all_to_all(request.reshape(owners, capacity), OWN, split_axis=0, conc...  13.6 us
    ppermute x8, starting transfers between devices, send(): return lax.ppermute(x, 'tp', [(i, (i + step) % size) for i in range(size)])  13.3 us
    pallas_call x3, Pallas kernels, scatter_rows(): pl.pallas_call(body, out_shape=jax.ShapeDtypeStruct((cells, rows, width),...  9.28 us
    pallas_call x3, Pallas kernels, gather_rows(): pl.pallas_call(body, out_shape=jax.ShapeDtypeStruct((count, rows, width),...  9.16 us
  transfers between devices with their start and end apart: 12, of which 3 were waited for; matrix products, arithmetic and copies ran while one was open for 2% of the time, Pallas kernels for 19%

profile of v3, /device:TPU:2, one launch (start us, length us, event | category | flops | bytes accessed | tf_op | source)
XLA Modules:
  0.0 252.7 jit_solution(14883303141021617366)
XLA Ops:
  6.5 0.7 fusion
  7.2 0.9 convert_reduce_fusion
  8.3 13.6 %all_to_all.21 = s32[32,1,2]{2,1,0:T(1,128)S(1)} all-to-all(s32[32,1,2]{2,1,0:T(1,128)S(1)} %bitcast.40), channel_id=1, replica_groups=mesh['section'=4,'seq'=8,'tp'=4] {'section','seq'}, dimensions={0} | all-to-all | bytes 512 | tf_op jit(solution)/shard_map/all_to_all | solution.py:241
  22.4 0.7 reduce.3
  23.2 0.6 select_reduce_fusion.position_ref
  23.8 3.4 %pick_rows.3 = bf16[64,32,1024]{2,1,0:T(8,128)(2,1)} custom-call(s32[24]{0:T(128)} %select_reduce_fusion.position_ref, bf16[24,64,1024]{2,1,0:T(8,128)(2,1)} %bitcast.21), custom_call_target="tpu_custom_call" | custom-call | bytes 3145728 | tf_op jit(solution)/shard_map/pick_rows/pallas_call | solution.py:36
  27.3 5.9 %all-to-all-start.1 = ((bf16[32,2,32,1024]{3,2,1,0:T(8,128)(2,1)}), bf16[32,2,32,1024]{3,2,1,0:T(8,128)(2,1)}, u32[]{:S(2)}, u32[]{:S(2)}) async-start(bf16[32,2,32,1024]{3,2,1,0:T(8,128)(2,1)} %bitcast.24), calls=%async_computation.1 | async-start | bytes 8388608 | tf_op jit(solution)/shard_map/all_to_all | solution.py:273
  33.2 2.9 %pick_rows.4 = bf16[64,16,1024]{2,1,0:T(8,128)(2,1)} custom-call(s32[24]{0:T(128)} %select_reduce_fusion.position_ref, bf16[24,64,1024]{2,1,0:T(8,128)(2,1)} %bitcast.22), custom_call_target="tpu_custom_call" | custom-call | bytes 1572864 | tf_op jit(solution)/shard_map/pick_rows/pallas_call | solution.py:36
  36.2 2.9 %pick_rows.5 = bf16[64,16,1024]{2,1,0:T(8,128)(2,1)} custom-call(s32[24]{0:T(128)} %select_reduce_fusion.position_ref, bf16[24,64,1024]{2,1,0:T(8,128)(2,1)} %bitcast.23), custom_call_target="tpu_custom_call" | custom-call | bytes 1572864 | tf_op jit(solution)/shard_map/pick_rows/pallas_call | solution.py:36
  39.1 45.6 %all-to-all-done.1 = bf16[32,2,32,1024]{3,2,1,0:T(8,128)(2,1)} async-done(((bf16[32,2,32,1024]{3,2,1,0:T(8,128)(2,1)}), bf16[32,2,32,1024]{3,2,1,0:T(8,128)(2,1)}, u32[]{:S(2)}, u32[]{:S(2)}) %all-to-all-start.1) | async-done | bytes 4194336 | tf_op jit(solution)/shard_map/all_to_all | solution.py:273
  84.7 3.4 %place_rows.3 = bf16[24,32,1024]{2,1,0:T(8,128)(2,1)} custom-call(s32[24]{0:T(128)} %copy-done.3, bf16[64,32,1024]{2,1,0:T(8,128)(2,1)} %bitcast.9.cells_ref), custom_call_target="tpu_custom_call" | custom-call | bytes 3145728 | tf_op jit(solution)/shard_map/place_rows/pallas_call | solution.py:68
  88.1 6.1 %all-to-all-start.3 = ((bf16[32,2,16,1024]{3,2,1,0:T(8,128)(2,1)}), bf16[32,2,16,1024]{3,2,1,0:T(8,128)(2,1)S(1)}, u32[]{:S(2)}, u32[]{:S(2)}) async-start(bf16[32,2,16,1024]{3,2,1,0:T(8,128)(2,1)} %bitcast.25), calls=%async_computation.3 | async-start | bytes 4194304 | tf_op jit(solution)/shard_map/all_to_all | solution.py:273
  94.2 28.0 %all-to-all-done.3 = bf16[32,2,16,1024]{3,2,1,0:T(8,128)(2,1)S(1)} async-done(((bf16[32,2,16,1024]{3,2,1,0:T(8,128)(2,1)}), bf16[32,2,16,1024]{3,2,1,0:T(8,128)(2,1)S(1)}, u32[]{:S(2)}, u32[]{:S(2)}) %all-to-all-start.3) | async-done | bytes 2097184 | tf_op jit(solution)/shard_map/all_to_all | solution.py:273
  122.2 1.3 copy-done
  123.6 6.7 %all-to-all-start.2 = ((bf16[32,2,16,1024]{3,2,1,0:T(8,128)(2,1)}), bf16[32,2,16,1024]{3,2,1,0:T(8,128)(2,1)}, u32[]{:S(2)}, u32[]{:S(2)}) async-start(bf16[32,2,16,1024]{3,2,1,0:T(8,128)(2,1)} %bitcast.8), calls=%async_computation.2 | async-start | bytes 4194304 | tf_op jit(solution)/shard_map/all_to_all | solution.py:273
  130.3 2.9 %place_rows.4 = bf16[24,16,1024]{2,1,0:T(8,128)(2,1)} custom-call(s32[24]{0:T(128)} %copy-done.3, bf16[64,16,1024]{2,1,0:T(8,128)(2,1)} %bitcast.26), custom_call_target="tpu_custom_call" | custom-call | bytes 1572864 | tf_op jit(solution)/shard_map/place_rows/pallas_call | solution.py:68
  133.1 2.0 collective-permute-start
  135.1 2.2 collective-permute-start.1
  137.3 33.0 %collective-permute-done.refs_1_ = bf16[384,1024]{1,0:T(8,128)(2,1)S(1)} collective-permute-done((bf16[384,1024]{1,0:T(8,128)(2,1)}, bf16[384,1024]{1,0:T(8,128)(2,1)S(1)}, u32[]{:S(2)}, u32[]{:S(2)}) %collective-permute-start) | collective-permute-done | bytes 786464 | tf_op jit(solution)/shard_map/ppermute | solution.py:90
  170.5 0.8 copy-done.1
  171.3 0.9 copy-done.2
  172.2 0.8 slice.17
  172.9 2.4 collective-permute-start.3
  175.4 2.9 %place_rows.5 = bf16[24,16,1024]{2,1,0:T(8,128)(2,1)} custom-call(s32[24]{0:T(128)} %copy-done.3, bf16[64,16,1024]{2,1,0:T(8,128)(2,1)} %bitcast.13.cells_ref), custom_call_target="tpu_custom_call" | custom-call | bytes 1572864 | tf_op jit(solution)/shard_map/place_rows/pallas_call | solution.py:68
  178.3 3.2 %collective-permute-start.5 = (bf16[384,1024]{1,0:T(8,128)(2,1)}, bf16[384,1024]{1,0:T(8,128)(2,1)}, u32[]{:S(2)}, u32[]{:S(2)}) collective-permute-start(bf16[384,1024]{1,0:T(8,128)(2,1)} %bitcast.34), channel_id=1, source_target_pairs={{0,3},{1,0},{2,1},{3,2},{4,7},{5,4},{6,5},{7,6},{8,11},{9,8},{10,9... | collective-permute-start | bytes 2359304 | tf_op jit(solution)/shard_map/ppermute | solution.py:90
  181.6 23.0 %norm_and_project.3 = (bf16[768,1024]{1,0:T(8,128)(2,1)}, bf16[768,1024]{1,0:T(8,128)(2,1)}) custom-call(s32[1]{0:T(128)} %bitcast.here_ref, f32[1,4096]{1,0:T(1,128)} %bitcast.47, bf16[4096,1024]{1,0:T(8,128)(2,1)} %bitcast.41, bf16[4096,1024]{1,0:T(8,128)(2,1)} %bitcast.44, bf16[4,768,1024]{2,1,0:T(8,128)(2,1)} %all-gather.2.cloned.1.call-done.refs_0_), custom_call_target="tpu_custom_call" | custom-call | flops 12884901888 | bytes 23068672 | tf_op jit(solution)/shard_map/norm_and_project/pallas_call | solution.py:146
  204.6 1.8 slice.14
  206.4 1.8 slice.15
  208.1 3.2 %collective-permute-start.7 = (bf16[192,1024]{1,0:T(8,128)(2,1)}, bf16[192,1024]{1,0:T(8,128)(2,1)}, u32[]{:S(2)}, u32[]{:S(2)}) collective-permute-start(bf16[192,1024]{1,0:T(8,128)(2,1)} %slice.15), channel_id=1, source_target_pairs={{0,3},{1,0},{2,1},{3,2},{4,7},{5,4},{6,5},{7,6},{8,11},{9,8},{10,9... | collective-permute-start | bytes 1179656 | tf_op jit(solution)/shard_map/ppermute | solution.py:90
  211.4 14.1 %norm_and_project.4 = (bf16[384,1024]{1,0:T(8,128)(2,1)}, bf16[384,1024]{1,0:T(8,128)(2,1)}) custom-call(s32[1]{0:T(128)} %bitcast.here_ref, f32[1,4096]{1,0:T(1,128)} %bitcast.48, bf16[4096,1024]{1,0:T(8,128)(2,1)} %bitcast.42, bf16[4096,1024]{1,0:T(8,128)(2,1)} %bitcast.45, bf16[384,1024]{1,0:T(8,128)(2,1)} %bitcast.32, bf16[384,1024]{1,0:T(8,128)(2,1)} %copy-done.1, ...), custom_call_target="tpu_custom_call" | custom-call | flops 6442450944 | bytes 19922944 | tf_op jit(solution)/shard_map/norm_and_project/pallas_call | solution.py:146
  225.5 14.1 %norm_and_project.5 = (bf16[384,1024]{1,0:T(8,128)(2,1)}, bf16[384,1024]{1,0:T(8,128)(2,1)}) custom-call(s32[1]{0:T(128)} %bitcast.here_ref, f32[1,4096]{1,0:T(1,128)} %bitcast.49, bf16[4096,1024]{1,0:T(8,128)(2,1)} %bitcast.43, bf16[4096,1024]{1,0:T(8,128)(2,1)} %bitcast.46, bf16[384,1024]{1,0:T(8,128)(2,1)} %bitcast.35, ...), custom_call_target="tpu_custom_call" | custom-call | flops 6442450944 | bytes 19922944 | tf_op jit(solution)/shard_map/norm_and_project/pallas_call | solution.py:146
  239.6 6.2 %attention.1 = bf16[384,1024]{1,0:T(8,128)(2,1)} custom-call(s32[6]{0:T(128)} %count_ref.1, bf16[384,1024]{1,0:T(8,128)(2,1)} %query_ref.1, bf16[6,128,1024]{2,1,0:T(8,128)(2,1)} %bitcast.28, bf16[6,64,1024]{2,1,0:T(8,128)(2,1)} %bitcast.36, bf16[6,64,1024]{2,1,0:T(8,128)(2,1)} %bitcast.38, bf16[6,128,1024]{2,1,0:T(8,128)(2,1)} %bitcast.29, ...), custom_call_target="tpu_custom_call" | custom-call | flops 402653184 | bytes 7864320 | tf_op jit(solution)/shard_map/attention/pallas_call | solution.py:210
  (26 shorter events, 1.1 us)
Async XLA Ops:
  8.1 19.2 %copy-start.3 = (s32[24]{0:T(128)}, s32[24]{0:T(128)S(1)}, u32[]{:S(2)}) copy-start(s32[24]{0:T(128)S(1)} %multiply_add_fusion.position_ref) | copy-start | bytes 292
  27.3 57.4 %all-to-all-start.1 = ((bf16[32,2,32,1024]{3,2,1,0:T(8,128)(2,1)}), bf16[32,2,32,1024]{3,2,1,0:T(8,128)(2,1)}, u32[]{:S(2)}, u32[]{:S(2)}) async-start(bf16[32,2,32,1024]{3,2,1,0:T(8,128)(2,1)} %bitcast.24), calls=%async_computation.1 | async-start | bytes 8388608 | tf_op jit(solution)/shard_map/all_to_all | solution.py:273
  33.2 148.4 %all-gather.2.cloned.1.call-start = ((), (), s32[]{:S(2)}) async-start(), calls=%async_computation.4 | async-start | bytes 7864320 | tf_op jit(solution)/shard_map/all_gather | solution.py:283
  88.1 34.1 %all-to-all-start.3 = ((bf16[32,2,16,1024]{3,2,1,0:T(8,128)(2,1)}), bf16[32,2,16,1024]{3,2,1,0:T(8,128)(2,1)S(1)}, u32[]{:S(2)}, u32[]{:S(2)}) async-start(bf16[32,2,16,1024]{3,2,1,0:T(8,128)(2,1)} %bitcast.25), calls=%async_computation.3 | async-start | bytes 4194304 | tf_op jit(solution)/shard_map/all_to_all | solution.py:273
  122.2 1.3 copy-start
  123.6 51.8 %all-to-all-start.2 = ((bf16[32,2,16,1024]{3,2,1,0:T(8,128)(2,1)}), bf16[32,2,16,1024]{3,2,1,0:T(8,128)(2,1)}, u32[]{:S(2)}, u32[]{:S(2)}) async-start(bf16[32,2,16,1024]{3,2,1,0:T(8,128)(2,1)} %bitcast.8), calls=%async_computation.2 | async-start | bytes 4194304 | tf_op jit(solution)/shard_map/all_to_all | solution.py:273
  133.1 37.2 %collective-permute-start = (bf16[384,1024]{1,0:T(8,128)(2,1)}, bf16[384,1024]{1,0:T(8,128)(2,1)S(1)}, u32[]{:S(2)}, u32[]{:S(2)}) collective-permute-start(bf16[384,1024]{1,0:T(8,128)(2,1)} %bitcast.30), channel_id=1, source_target_pairs={{0,1},{1,2},{2,3},{3,0},{4,5},{5,6},{6,7},{7,4},{8,9},{9,10},{10,1... | collective-permute-start | bytes 2359304 | tf_op jit(solution)/shard_map/ppermute | solution.py:90
  135.1 36.2 %collective-permute-start.1 = (bf16[384,1024]{1,0:T(8,128)(2,1)}, bf16[384,1024]{1,0:T(8,128)(2,1)S(1)}, u32[]{:S(2)}, u32[]{:S(2)}) collective-permute-start(bf16[384,1024]{1,0:T(8,128)(2,1)} %bitcast.31), channel_id=1, source_target_pairs={{0,3},{1,0},{2,1},{3,2},{4,7},{5,4},{6,5},{7,6},{8,11},{9,8},{10,9... | collective-permute-start | bytes 2359304 | tf_op jit(solution)/shard_map/ppermute | solution.py:90
  170.4 0.9 copy-start.1
  170.4 41.0 %collective-permute-start.2 = (bf16[192,1024]{1,0:T(8,128)(2,1)S(1)}, bf16[192,1024]{1,0:T(8,128)(2,1)}, u32[]{:S(2)}, u32[]{:S(2)}) collective-permute-start(bf16[192,1024]{1,0:T(8,128)(2,1)S(1)} %slice.16), channel_id=1, source_target_pairs={{0,1},{1,2},{2,3},{3,0},{4,5},{5,6},{6,7},{7,4},{8,9},{9,10},{10,1... | collective-permute-start | bytes 1179656 | tf_op jit(solution)/shard_map/ppermute | solution.py:90
  171.3 0.9 copy-start.2
  172.9 38.4 %collective-permute-start.3 = (bf16[192,1024]{1,0:T(8,128)(2,1)}, bf16[192,1024]{1,0:T(8,128)(2,1)}, u32[]{:S(2)}, u32[]{:S(2)}) collective-permute-start(bf16[192,1024]{1,0:T(8,128)(2,1)} %slice.17), channel_id=1, source_target_pairs={{0,3},{1,0},{2,1},{3,2},{4,7},{5,4},{6,5},{7,6},{8,11},{9,8},{10,9... | collective-permute-start | bytes 1179656 | tf_op jit(solution)/shard_map/ppermute | solution.py:90
  178.2 26.4 %collective-permute-start.4 = (bf16[384,1024]{1,0:T(8,128)(2,1)}, bf16[384,1024]{1,0:T(8,128)(2,1)}, u32[]{:S(2)}, u32[]{:S(2)}) collective-permute-start(bf16[384,1024]{1,0:T(8,128)(2,1)} %bitcast.33), channel_id=1, source_target_pairs={{0,1},{1,2},{2,3},{3,0},{4,5},{5,6},{6,7},{7,4},{8,9},{9,10},{10,1... | collective-permute-start | bytes 2359304 | tf_op jit(solution)/shard_map/ppermute | solution.py:90
  178.3 26.3 %collective-permute-start.5 = (bf16[384,1024]{1,0:T(8,128)(2,1)}, bf16[384,1024]{1,0:T(8,128)(2,1)}, u32[]{:S(2)}, u32[]{:S(2)}) collective-permute-start(bf16[384,1024]{1,0:T(8,128)(2,1)} %bitcast.34), channel_id=1, source_target_pairs={{0,3},{1,0},{2,1},{3,2},{4,7},{5,4},{6,5},{7,6},{8,11},{9,8},{10,9... | collective-permute-start | bytes 2359304 | tf_op jit(solution)/shard_map/ppermute | solution.py:90
  208.1 17.4 %collective-permute-start.6 = (bf16[192,1024]{1,0:T(8,128)(2,1)}, bf16[192,1024]{1,0:T(8,128)(2,1)}, u32[]{:S(2)}, u32[]{:S(2)}) collective-permute-start(bf16[192,1024]{1,0:T(8,128)(2,1)} %slice.14), channel_id=1, source_target_pairs={{0,1},{1,2},{2,3},{3,0},{4,5},{5,6},{6,7},{7,4},{8,9},{9,10},{10,1... | collective-permute-start | bytes 1179656 | tf_op jit(solution)/shard_map/ppermute | solution.py:90
  208.1 17.4 %collective-permute-start.7 = (bf16[192,1024]{1,0:T(8,128)(2,1)}, bf16[192,1024]{1,0:T(8,128)(2,1)}, u32[]{:S(2)}, u32[]{:S(2)}) collective-permute-start(bf16[192,1024]{1,0:T(8,128)(2,1)} %slice.15), channel_id=1, source_target_pairs={{0,3},{1,0},{2,1},{3,2},{4,7},{5,4},{6,5},{7,6},{8,11},{9,8},{10,9... | collective-permute-start | bytes 1179656 | tf_op jit(solution)/shard_map/ppermute | solution.py:90
Sparse Core Ops, SparseCore 0:
  88.3 80.7 all-gather.1

commit v4 on v1

--- a/solution.py
+++ b/solution.py
@@ -11,10 +11,10 @@
 PIECE = 64
 NBR = 2
 CHUNKS = (16, 16, 16, 16)
-MODE = ("offload", "ring", "offload", "ring")
+MODE = ("offload", "offload", "ring", "ring")
 EPS = 1e-05
 OWN = ("section", "seq")
-KERNEL_VMEM = 62 << 20
+KERNEL_VMEM = 127 << 19
 
 
 def scatter_rows(position, pieces, offset, rows, cells):
@@ -53,17 +53,20 @@
     count = position.shape[0]
     _, rows, width = cells.shape
 
-    def body(position_ref, cells_ref, out_ref, held, sem, sems):
+    def body(position_ref, cells_ref, out_ref, held, stored, sems):
         def copy(t):
             return pltpu.make_async_copy(cells_ref.at[position_ref[t]], held.at[t], sems.at[t])
 
         for t in range(count):
             copy(t).start()
+        def store(t):
+            return pltpu.make_async_copy(held.at[t], out_ref.at[t], stored.at[t])
+
         for t in range(count):
             copy(t).wait()
-        store = pltpu.make_async_copy(held, out_ref, sem)
-        store.start()
-        store.wait()
+            store(t).start()
+        for t in range(count):
+            store(t).wait()
 
     return pl.pallas_call(
         body,
@@ -72,7 +75,7 @@
         out_specs=pl.BlockSpec(memory_space=pl.ANY),
         scratch_shapes=[
             pltpu.VMEM((count, rows, width), cells.dtype),
-            pltpu.SemaphoreType.DMA,
+            pltpu.SemaphoreType.DMA((count,)),
             pltpu.SemaphoreType.DMA((count,)),
         ],
         compiler_params=pltpu.CompilerParams(vmem_limit_bytes=KERNEL_VMEM),
@@ -115,7 +118,7 @@
                         return slice(step[0] * width, (step[0] + 1) * width)
                     return pl.ds(pl.multiple_of((here_ref[0] + step) % size * width, width), width)
 
-                @pl.loop(0, (last - first) // block, unroll=2)
+                @pl.loop(0, (last - first) // block, unroll=4)
                 def _(b):
                     at = pl.multiple_of(first + b * block, block)
                     total = jnp.zeros((block, HD), jnp.float32)
@@ -270,12 +273,12 @@
         ready = picked[j]
         if j >= 2:
             ready = after(ready, parts[j - 2][0][2])
+        if j == 3:
+            finish(0)
+            ready = after(ready, done[0][0])
         arrived = lax.all_to_all(ready, OWN, split_axis=0, concat_axis=0, tiled=True)
         if j == 0:
             arrived = after(arrived, *picked[1:])
-        if j >= 3:
-            finish(j - 3)
-            arrived = after(arrived, done[j - 3][0])
         if j - 1 in halves:
             arrived = after(arrived, *halves[j - 1])
         own = place(j, arrived)
@@ -284,12 +287,14 @@
             parts.append([(0, 0, own), (None, 0, full)])
             continue
         up, down = send(own, 1), send(own, size - 1)
+        if j >= 2:
+            parts[j - 1][-1] = parts[j - 1][-1][:2] + (after(parts[j - 1][-1][2], own),)
+            finish(j - 1)
+            up, down = lax.optimization_barrier((up, down, done[j - 1][0]))[:2]
         half = own.shape[0] // 2
         halves[j] = up[:half], down[half:]
         far = send(halves[j][0], 1), send(halves[j][1], size - 1)
         parts.append([(0, 0, own), (size - 1, 0, up), (1, 0, down), (2, 0, far[0]), (2, half, far[1])])
-    parts[-2][-1] = parts[-2][-1][:2] + (after(parts[-2][-1][2], *halves[count - 1]),)
-    parts[-3][-1] = parts[-3][-1][:2] + (after(parts[-3][-1][2], parts[-1][0][2]),)
     for j in range(count):
         if j not in done:
             finish(j)

time: 247 us -> 241 us (0.976)
  blocking collectives: 13.6 us -> 47.8 us
  waiting for transfers between devices: 82.4 us -> 53.3 us
  starting transfers between devices: 41.3 us -> 32.6 us
  Pallas kernels: 85.9 us -> 83.2 us
    all_to_all x0 -> x1, blocking collectives: none -> 34.2 us  [per_device(): lax.all_to_all(ready, OWN, split_axis=0, concat_axis=0, tiled=True)]
    all_to_all x4 -> x3, waiting for transfers between devices: 58.6 us -> 33.4 us  [per_device(): lax.all_to_all(ready, OWN, split_axis=0, concat_axis=0, tiled=True)]
    all_to_all x4 -> x3, starting transfers between devices: 25.3 us -> 18.3 us  [per_device(): lax.all_to_all(ready, OWN, split_axis=0, concat_axis=0, tiled=True)]
    ppermute x8, waiting for transfers between devices: 23.7 us -> 19.8 us  [send(): return lax.ppermute(x, 'tp', [(i, (i + step) % size) for i in range(size)])]
    slice x4, local copies, waits for them, and re-layouts: 1.27 us -> 4.84 us  [per_device(): halves[j] = (up[:half], down[half:])]
    unnamed x14 -> x4, local copies, waits for them, and re-layouts: 3.76 us -> 0.21 us
  transfers between devices with their start and end apart: 14 -> 13, of which waited for: 6 -> 8; matrix products, arithmetic and copies ran while one was open for 1% -> 2% of each run, Pallas kernels for 24% -> 24%
where the time goes in v4:
time: 241 us; the launch traced here: 239 us
  Pallas kernels  83.2 us (35%)
  waiting for transfers between devices  53.3 us (22%)
  blocking collectives  47.8 us (20%)
  starting transfers between devices  32.6 us (14%)
  between operations  13.6 us (6%)
  local copies, waits for them, and re-layouts  5.76 us (2%)
  other arithmetic  3.01 us (1%)
    pallas_call x4, Pallas kernels, project(): pl.pallas_call(body, grid=(columns // tile,), out_shape=(out, out), in_sp...  54.1 us
    all_to_all x1, blocking collectives, per_device(): lax.all_to_all(ready, OWN, split_axis=0, concat_axis=0, tiled=True)  34.2 us
    all_to_all x3, waiting for transfers between devices, per_device(): lax.all_to_all(ready, OWN, split_axis=0, concat_axis=0, tiled=True)  33.4 us
    ppermute x8, waiting for transfers between devices, send(): return lax.ppermute(x, 'tp', [(i, (i + step) % size) for i in range(size)])  19.8 us
    all_to_all x3, starting transfers between devices, per_device(): lax.all_to_all(ready, OWN, split_axis=0, concat_axis=0, tiled=True)  18.3 us
    ppermute x8, starting transfers between devices, send(): return lax.ppermute(x, 'tp', [(i, (i + step) % size) for i in range(size)])  14.2 us
    all_to_all x1, blocking collectives, per_device(): lax.all_to_all(request.reshape(owners, capacity), OWN, split_axis=0, conc...  13.6 us
    pallas_call x4, Pallas kernels, scatter_rows(): pl.pallas_call(body, out_shape=jax.ShapeDtypeStruct((cells, rows, width),...  11.6 us
  transfers between devices with their start and end apart: 13, of which 8 were waited for; matrix products, arithmetic and copies ran while one was open for 2% of the time, Pallas kernels for 24%

profile of v4, /device:TPU:2, one launch (start us, length us, event | category | flops | bytes accessed | tf_op | source)
XLA Modules:
  0.0 239.2 jit_solution(6664471415370774395)
XLA Ops:
  8.3 13.6 %all_to_all.26 = s32[32,1,2]{2,1,0:T(1,128)S(1)} all-to-all(s32[32,1,2]{2,1,0:T(1,128)S(1)} %bitcast.51), channel_id=1, replica_groups=mesh['section'=4,'seq'=8,'tp'=4] {'section','seq'}, dimensions={0} | all-to-all | bytes 512 | tf_op jit(solution)/shard_map/all_to_all | solution.py:244
  23.8 2.9 %pick_rows.4 = bf16[64,16,1024]{2,1,0:T(8,128)(2,1)} custom-call(s32[24]{0:T(128)} %select_reduce_fusion.position_ref, bf16[24,64,1024]{2,1,0:T(8,128)(2,1)} %bitcast.26), custom_call_target="tpu_custom_call" | custom-call | bytes 1572864 | tf_op jit(solution)/shard_map/pick_rows/pallas_call | solution.py:36
  26.8 5.8 %all-to-all-start.1 = ((bf16[32,2,16,1024]{3,2,1,0:T(8,128)(2,1)}), bf16[32,2,16,1024]{3,2,1,0:T(8,128)(2,1)}, u32[]{:S(2)}, u32[]{:S(2)}) async-start(bf16[32,2,16,1024]{3,2,1,0:T(8,128)(2,1)} %bitcast.33), calls=%async_computation.1 | async-start | bytes 4194304 | tf_op jit(solution)/shard_map/all_to_all | solution.py:279
  32.6 2.9 %pick_rows.5 = bf16[64,16,1024]{2,1,0:T(8,128)(2,1)} custom-call(s32[24]{0:T(128)} %select_reduce_fusion.position_ref, bf16[24,64,1024]{2,1,0:T(8,128)(2,1)} %bitcast.27), custom_call_target="tpu_custom_call" | custom-call | bytes 1572864 | tf_op jit(solution)/shard_map/pick_rows/pallas_call | solution.py:36
  35.5 2.9 %pick_rows.6 = bf16[64,16,1024]{2,1,0:T(8,128)(2,1)} custom-call(s32[24]{0:T(128)} %select_reduce_fusion.position_ref, bf16[24,64,1024]{2,1,0:T(8,128)(2,1)} %bitcast.28), custom_call_target="tpu_custom_call" | custom-call | bytes 1572864 | tf_op jit(solution)/shard_map/pick_rows/pallas_call | solution.py:36
  38.5 2.9 %pick_rows.7 = bf16[64,16,1024]{2,1,0:T(8,128)(2,1)} custom-call(s32[24]{0:T(128)} %select_reduce_fusion.position_ref, bf16[24,64,1024]{2,1,0:T(8,128)(2,1)} %bitcast.29), custom_call_target="tpu_custom_call" | custom-call | bytes 1572864 | tf_op jit(solution)/shard_map/pick_rows/pallas_call | solution.py:36
  41.4 19.2 %all-to-all-done.1 = bf16[32,2,16,1024]{3,2,1,0:T(8,128)(2,1)} async-done(((bf16[32,2,16,1024]{3,2,1,0:T(8,128)(2,1)}), bf16[32,2,16,1024]{3,2,1,0:T(8,128)(2,1)}, u32[]{:S(2)}, u32[]{:S(2)}) %all-to-all-start.1) | async-done | bytes 2097184 | tf_op jit(solution)/shard_map/all_to_all | solution.py:279
  60.6 2.8 %place_rows.4 = bf16[24,16,1024]{2,1,0:T(8,128)(2,1)} custom-call(s32[24]{0:T(128)} %copy-done, bf16[64,16,1024]{2,1,0:T(8,128)(2,1)} %bitcast.10.cells_ref), custom_call_target="tpu_custom_call" | custom-call | bytes 1572864 | tf_op jit(solution)/shard_map/place_rows/pallas_call | solution.py:71
  63.5 34.2 %all_to_all.27 = bf16[32,2,16,1024]{3,2,1,0:T(8,128)(2,1)} all-to-all(bf16[32,2,16,1024]{3,2,1,0:T(8,128)(2,1)} %bitcast.32), channel_id=1, replica_groups=mesh['section'=4,'seq'=8,'tp'=4] {'section','seq'}, dimensions={0} | all-to-all | bytes 4194304 | tf_op jit(solution)/shard_map/all_to_all | solution.py:279
  97.7 2.8 %place_rows.5 = bf16[24,16,1024]{2,1,0:T(8,128)(2,1)} custom-call(s32[24]{0:T(128)} %copy-done, bf16[64,16,1024]{2,1,0:T(8,128)(2,1)} %bitcast.34), custom_call_target="tpu_custom_call" | custom-call | bytes 1572864 | tf_op jit(solution)/shard_map/place_rows/pallas_call | solution.py:71
  100.6 5.8 %all-to-all-start.3 = ((bf16[32,2,16,1024]{3,2,1,0:T(8,128)(2,1)}), bf16[32,2,16,1024]{3,2,1,0:T(8,128)(2,1)}, u32[]{:S(2)}, u32[]{:S(2)}) async-start(bf16[32,2,16,1024]{3,2,1,0:T(8,128)(2,1)} %bitcast.31), calls=%async_computation.3 | async-start | bytes 4194304 | tf_op jit(solution)/shard_map/all_to_all | solution.py:279
  106.4 13.8 %norm_and_project.4 = (bf16[384,1024]{1,0:T(8,128)(2,1)}, bf16[384,1024]{1,0:T(8,128)(2,1)}) custom-call(s32[1]{0:T(128)} %bitcast.here_ref, f32[1,4096]{1,0:T(1,128)} %bitcast.60, bf16[4096,1024]{1,0:T(8,128)(2,1)} %bitcast.52, bf16[4096,1024]{1,0:T(8,128)(2,1)} %bitcast.56, bf16[4,384,1024]{2,1,0:T(8,128)(2,1)} %all-gather.3.cloned.1.call-done.refs_0_), custom_call_target="tpu_custom_call" | custom-call | flops 6442450944 | bytes 19922944 | tf_op jit(solution)/shard_map/norm_and_project/pallas_call | solution.py:149
  120.2 14.2 %all-to-all-done.3 = bf16[32,2,16,1024]{3,2,1,0:T(8,128)(2,1)} async-done(((bf16[32,2,16,1024]{3,2,1,0:T(8,128)(2,1)}), bf16[32,2,16,1024]{3,2,1,0:T(8,128)(2,1)}, u32[]{:S(2)}, u32[]{:S(2)}) %all-to-all-start.3) | async-done | bytes 2097184 | tf_op jit(solution)/shard_map/all_to_all | solution.py:279
  134.4 6.7 %all-to-all-start.4 = ((bf16[32,2,16,1024]{3,2,1,0:T(8,128)(2,1)}), bf16[32,2,16,1024]{3,2,1,0:T(8,128)(2,1)}, u32[]{:S(2)}, u32[]{:S(2)}) async-start(bf16[32,2,16,1024]{3,2,1,0:T(8,128)(2,1)} %bitcast.30), calls=%async_computation.4 | async-start | bytes 4194304 | tf_op jit(solution)/shard_map/all_to_all | solution.py:279
  141.1 2.8 %place_rows.6 = bf16[24,16,1024]{2,1,0:T(8,128)(2,1)} custom-call(s32[24]{0:T(128)} %copy-done, bf16[64,16,1024]{2,1,0:T(8,128)(2,1)} %bitcast.15.cells_ref), custom_call_target="tpu_custom_call" | custom-call | bytes 1572864 | tf_op jit(solution)/shard_map/place_rows/pallas_call | solution.py:71
  143.9 2.0 collective-permute-start
  145.9 2.2 collective-permute-start.1
  148.1 13.5 %norm_and_project.5 = (bf16[384,1024]{1,0:T(8,128)(2,1)}, bf16[384,1024]{1,0:T(8,128)(2,1)}) custom-call(s32[1]{0:T(128)} %bitcast.here_ref, f32[1,4096]{1,0:T(1,128)} %bitcast.61, bf16[4096,1024]{1,0:T(8,128)(2,1)} %bitcast.53, bf16[4096,1024]{1,0:T(8,128)(2,1)} %bitcast.57, bf16[4,384,1024]{2,1,0:T(8,128)(2,1)} %all-gather.5.cloned.1.call-done.refs_0_), custom_call_target="tpu_custom_call" | custom-call | flops 6442450944 | bytes 19922944 | tf_op jit(solution)/shard_map/norm_and_project/pallas_call | solution.py:149
  161.6 4.6 %collective-permute-done.refs_1_ = bf16[384,1024]{1,0:T(8,128)(2,1)} collective-permute-done((bf16[384,1024]{1,0:T(8,128)(2,1)}, bf16[384,1024]{1,0:T(8,128)(2,1)}, u32[]{:S(2)}, u32[]{:S(2)}) %collective-permute-start) | collective-permute-done | bytes 786464 | tf_op jit(solution)/shard_map/ppermute | solution.py:93
  166.2 1.0 slice.13
  167.2 3.1 %collective-permute-start.3 = (bf16[192,1024]{1,0:T(8,128)(2,1)S(1)}, bf16[192,1024]{1,0:T(8,128)(2,1)}, u32[]{:S(2)}, u32[]{:S(2)}) collective-permute-start(bf16[192,1024]{1,0:T(8,128)(2,1)S(1)} %slice.13), channel_id=1, source_target_pairs={{0,3},{1,0},{2,1},{3,2},{4,7},{5,4},{6,5},{7,6},{8,11},{9,8},{10,9... | collective-permute-start | bytes 1179656 | tf_op jit(solution)/shard_map/ppermute | solution.py:93
  170.3 1.8 slice.12
  172.1 2.8 %place_rows.7 = bf16[24,16,1024]{2,1,0:T(8,128)(2,1)} custom-call(s32[24]{0:T(128)} %copy-done, bf16[64,16,1024]{2,1,0:T(8,128)(2,1)} %bitcast.18.cells_ref), custom_call_target="tpu_custom_call" | custom-call | bytes 1572864 | tf_op jit(solution)/shard_map/place_rows/pallas_call | solution.py:71
  175.2 3.1 %collective-permute-start.5 = (bf16[384,1024]{1,0:T(8,128)(2,1)}, bf16[384,1024]{1,0:T(8,128)(2,1)}, u32[]{:S(2)}, u32[]{:S(2)}) collective-permute-start(bf16[384,1024]{1,0:T(8,128)(2,1)} %bitcast.41), channel_id=1, source_target_pairs={{0,3},{1,0},{2,1},{3,2},{4,7},{5,4},{6,5},{7,6},{8,11},{9,8},{10,9... | collective-permute-start | bytes 2359304 | tf_op jit(solution)/shard_map/ppermute | solution.py:93
  179.0 6.7 %collective-permute-done.2.refs_3_ = bf16[192,1024]{1,0:T(8,128)(2,1)} collective-permute-done((bf16[192,1024]{1,0:T(8,128)(2,1)}, bf16[192,1024]{1,0:T(8,128)(2,1)}, u32[]{:S(2)}, u32[]{:S(2)}) %collective-permute-start.2) | collective-permute-done | bytes 393248 | tf_op jit(solution)/shard_map/ppermute | solution.py:93
  185.7 13.4 %norm_and_project.6 = (bf16[384,1024]{1,0:T(8,128)(2,1)}, bf16[384,1024]{1,0:T(8,128)(2,1)}) custom-call(s32[1]{0:T(128)} %bitcast.here_ref, f32[1,4096]{1,0:T(1,128)} %bitcast.62, bf16[4096,1024]{1,0:T(8,128)(2,1)} %bitcast.54, bf16[4096,1024]{1,0:T(8,128)(2,1)} %bitcast.58, bf16[384,1024]{1,0:T(8,128)(2,1)} %bitcast.39, ...), custom_call_target="tpu_custom_call" | custom-call | flops 6442450944 | bytes 19922944 | tf_op jit(solution)/shard_map/norm_and_project/pallas_call | solution.py:149
  199.1 1.4 collective-permute-done.4.refs_1_
  201.6 1.0 slice.15
  202.7 3.5 %collective-permute-start.7 = (bf16[192,1024]{1,0:T(8,128)(2,1)S(1)}, bf16[192,1024]{1,0:T(8,128)(2,1)}, u32[]{:S(2)}, u32[]{:S(2)}) collective-permute-start(bf16[192,1024]{1,0:T(8,128)(2,1)S(1)} %slice.15), channel_id=1, source_target_pairs={{0,3},{1,0},{2,1},{3,2},{4,7},{5,4},{6,5},{7,6},{8,11},{9,8},{10,9... | collective-permute-start | bytes 1179656 | tf_op jit(solution)/shard_map/ppermute | solution.py:93
  206.1 5.8 %collective-permute-done.6.refs_3_ = bf16[192,1024]{1,0:T(8,128)(2,1)S(1)} collective-permute-done((bf16[192,1024]{1,0:T(8,128)(2,1)S(1)}, bf16[192,1024]{1,0:T(8,128)(2,1)S(1)}, u32[]{:S(2)}, u32[]{:S(2)}) %collective-permute-start.6) | collective-permute-done | bytes 393248 | tf_op jit(solution)/shard_map/ppermute | solution.py:93
  212.7 13.4 %norm_and_project.7 = (bf16[384,1024]{1,0:T(8,128)(2,1)}, bf16[384,1024]{1,0:T(8,128)(2,1)}) custom-call(s32[1]{0:T(128)} %bitcast.here_ref, f32[1,4096]{1,0:T(1,128)} %bitcast.63, bf16[4096,1024]{1,0:T(8,128)(2,1)} %bitcast.55, bf16[4096,1024]{1,0:T(8,128)(2,1)} %bitcast.59, bf16[384,1024]{1,0:T(8,128)(2,1)} %bitcast.42, ...), custom_call_target="tpu_custom_call" | custom-call | flops 6442450944 | bytes 19922944 | tf_op jit(solution)/shard_map/norm_and_project/pallas_call | solution.py:149
  226.1 6.2 %attention.1 = bf16[384,1024]{1,0:T(8,128)(2,1)} custom-call(s32[6]{0:T(128)} %count_ref.1, bf16[384,1024]{1,0:T(8,128)(2,1)} %query_ref.1, bf16[6,64,1024]{2,1,0:T(8,128)(2,1)} %bitcast.43, bf16[6,64,1024]{2,1,0:T(8,128)(2,1)} %bitcast.45, bf16[6,64,1024]{2,1,0:T(8,128)(2,1)} %bitcast.47, bf16[6,64,1024]{2,1,0:T(8,128)(2,1)} %bitcast.49, ...), custom_call_target="tpu_custom_call" | custom-call | flops 402653184 | bytes 7864320 | tf_op jit(solution)/shard_map/attention/pallas_call | solution.py:213
  (29 shorter events, 6.7 us)
Async XLA Ops:
  8.1 18.6 %copy-start = (s32[24]{0:T(128)}, s32[24]{0:T(128)S(1)}, u32[]{:S(2)}) copy-start(s32[24]{0:T(128)S(1)} %multiply_add_fusion.position_ref) | copy-start | bytes 292
  26.8 33.9 %all-to-all-start.1 = ((bf16[32,2,16,1024]{3,2,1,0:T(8,128)(2,1)}), bf16[32,2,16,1024]{3,2,1,0:T(8,128)(2,1)}, u32[]{:S(2)}, u32[]{:S(2)}) async-start(bf16[32,2,16,1024]{3,2,1,0:T(8,128)(2,1)} %bitcast.33), calls=%async_computation.1 | async-start | bytes 4194304 | tf_op jit(solution)/shard_map/all_to_all | solution.py:279
  32.6 73.8 %all-gather.3.cloned.1.call-start = ((), (), s32[]{:S(2)}) async-start(), calls=%async_computation.5 | async-start | bytes 3932160 | tf_op jit(solution)/shard_map/all_gather | solution.py:286
  63.4 84.7 %all-gather.5.cloned.1.call-start = ((), (), s32[]{:S(2)}) async-start(), calls=%async_computation.6 | async-start | bytes 3932160 | tf_op jit(solution)/shard_map/all_gather | solution.py:286
  100.6 33.8 %all-to-all-start.3 = ((bf16[32,2,16,1024]{3,2,1,0:T(8,128)(2,1)}), bf16[32,2,16,1024]{3,2,1,0:T(8,128)(2,1)}, u32[]{:S(2)}, u32[]{:S(2)}) async-start(bf16[32,2,16,1024]{3,2,1,0:T(8,128)(2,1)} %bitcast.31), calls=%async_computation.3 | async-start | bytes 4194304 | tf_op jit(solution)/shard_map/all_to_all | solution.py:279
  134.4 37.7 %all-to-all-start.4 = ((bf16[32,2,16,1024]{3,2,1,0:T(8,128)(2,1)}), bf16[32,2,16,1024]{3,2,1,0:T(8,128)(2,1)}, u32[]{:S(2)}, u32[]{:S(2)}) async-start(bf16[32,2,16,1024]{3,2,1,0:T(8,128)(2,1)} %bitcast.30), calls=%async_computation.4 | async-start | bytes 4194304 | tf_op jit(solution)/shard_map/all_to_all | solution.py:279
  143.9 22.3 %collective-permute-start = (bf16[384,1024]{1,0:T(8,128)(2,1)}, bf16[384,1024]{1,0:T(8,128)(2,1)}, u32[]{:S(2)}, u32[]{:S(2)}) collective-permute-start(bf16[384,1024]{1,0:T(8,128)(2,1)} %bitcast.37), channel_id=1, source_target_pairs={{0,1},{1,2},{2,3},{3,0},{4,5},{5,6},{6,7},{7,4},{8,9},{9,10},{10,1... | collective-permute-start | bytes 2359304 | tf_op jit(solution)/shard_map/ppermute | solution.py:93
  145.9 20.3 %collective-permute-start.1 = (bf16[384,1024]{1,0:T(8,128)(2,1)}, bf16[384,1024]{1,0:T(8,128)(2,1)}, u32[]{:S(2)}, u32[]{:S(2)}) collective-permute-start(bf16[384,1024]{1,0:T(8,128)(2,1)} %bitcast.38), channel_id=1, source_target_pairs={{0,3},{1,0},{2,1},{3,2},{4,7},{5,4},{6,5},{7,6},{8,11},{9,8},{10,9... | collective-permute-start | bytes 2359304 | tf_op jit(solution)/shard_map/ppermute | solution.py:93
  167.2 11.8 %collective-permute-start.3 = (bf16[192,1024]{1,0:T(8,128)(2,1)S(1)}, bf16[192,1024]{1,0:T(8,128)(2,1)}, u32[]{:S(2)}, u32[]{:S(2)}) collective-permute-start(bf16[192,1024]{1,0:T(8,128)(2,1)S(1)} %slice.13), channel_id=1, source_target_pairs={{0,3},{1,0},{2,1},{3,2},{4,7},{5,4},{6,5},{7,6},{8,11},{9,8},{10,9... | collective-permute-start | bytes 1179656 | tf_op jit(solution)/shard_map/ppermute | solution.py:93
  172.1 13.6 %collective-permute-start.2 = (bf16[192,1024]{1,0:T(8,128)(2,1)}, bf16[192,1024]{1,0:T(8,128)(2,1)}, u32[]{:S(2)}, u32[]{:S(2)}) collective-permute-start(bf16[192,1024]{1,0:T(8,128)(2,1)} %slice.12), channel_id=1, source_target_pairs={{0,1},{1,2},{2,3},{3,0},{4,5},{5,6},{6,7},{7,4},{8,9},{9,10},{10,1... | collective-permute-start | bytes 1179656 | tf_op jit(solution)/shard_map/ppermute | solution.py:93
  174.9 25.6 %collective-permute-start.4 = (bf16[384,1024]{1,0:T(8,128)(2,1)}, bf16[384,1024]{1,0:T(8,128)(2,1)}, u32[]{:S(2)}, u32[]{:S(2)}) collective-permute-start(bf16[384,1024]{1,0:T(8,128)(2,1)} %bitcast.40), channel_id=1, source_target_pairs={{0,1},{1,2},{2,3},{3,0},{4,5},{5,6},{6,7},{7,4},{8,9},{9,10},{10,1... | collective-permute-start | bytes 2359304 | tf_op jit(solution)/shard_map/ppermute | solution.py:93
  175.2 25.3 %collective-permute-start.5 = (bf16[384,1024]{1,0:T(8,128)(2,1)}, bf16[384,1024]{1,0:T(8,128)(2,1)}, u32[]{:S(2)}, u32[]{:S(2)}) collective-permute-start(bf16[384,1024]{1,0:T(8,128)(2,1)} %bitcast.41), channel_id=1, source_target_pairs={{0,3},{1,0},{2,1},{3,2},{4,7},{5,4},{6,5},{7,6},{8,11},{9,8},{10,9... | collective-permute-start | bytes 2359304 | tf_op jit(solution)/shard_map/ppermute | solution.py:93
  201.6 10.4 %collective-permute-start.6 = (bf16[192,1024]{1,0:T(8,128)(2,1)S(1)}, bf16[192,1024]{1,0:T(8,128)(2,1)S(1)}, u32[]{:S(2)}, u32[]{:S(2)}) collective-permute-start(bf16[192,1024]{1,0:T(8,128)(2,1)S(1)} %slice.14), channel_id=1, source_target_pairs={{0,1},{1,2},{2,3},{3,0},{4,5},{5,6},{6,7},{7,4},{8,9},{9,10},{10,1... | collective-permute-start | bytes 1179656 | tf_op jit(solution)/shard_map/ppermute | solution.py:93
  202.7 9.8 %collective-permute-start.7 = (bf16[192,1024]{1,0:T(8,128)(2,1)S(1)}, bf16[192,1024]{1,0:T(8,128)(2,1)}, u32[]{:S(2)}, u32[]{:S(2)}) collective-permute-start(bf16[192,1024]{1,0:T(8,128)(2,1)S(1)} %slice.15), channel_id=1, source_target_pairs={{0,3},{1,0},{2,1},{3,2},{4,7},{5,4},{6,5},{7,6},{8,11},{9,8},{10,9... | collective-permute-start | bytes 1179656 | tf_op jit(solution)/shard_map/ppermute | solution.py:93
  212.0 0.7 copy-start.1
Sparse Core Ops, SparseCore 0:
  63.6 39.5 all-gather.2
  104.8 39.7 all-gather.4

commit v5 on v4

--- a/solution.py
+++ b/solution.py
@@ -176,7 +176,7 @@
     span = sum(spans)
     n = len(keys)
 
-    per = 2
+    per = 3
 
     def body(count_ref, query_ref, *refs):
         key_refs, value_refs, out_ref = refs[:n], refs[n : 2 * n], refs[2 * n]
@@ -203,7 +203,7 @@
             scores = jnp.concatenate(scores, 0) * HD ** (-0.5)
             scores = jnp.where(kept, scores, -1e30)
             exponents = jnp.exp(scores - jnp.max(scores, -1, keepdims=True))
-            weights = (exponents / jnp.sum(exponents, -1, keepdims=True)).astype(jnp.bfloat16)
+            weights = (exponents * (1.0 / jnp.sum(exponents, -1, keepdims=True))).astype(jnp.bfloat16)
             for h, a in enumerate(at):
                 v = jnp.concatenate([r[c, :, a] for r in value_refs], 0)
                 out_ref[row, a] = jnp.dot(

time: 241 us -> 240 us (level)
  no operation moved by 1% of the time
where the time goes in v5:
time: 240 us; the launch traced here: 239 us
  Pallas kernels  83 us (35%)
  waiting for transfers between devices  53.2 us (22%)
  blocking collectives  47.8 us (20%)
  starting transfers between devices  32.6 us (14%)
  between operations  13.6 us (6%)
  local copies, waits for them, and re-layouts  5.76 us (2%)
  other arithmetic  3.01 us (1%)
    pallas_call x4, Pallas kernels, project(): pl.pallas_call(body, grid=(columns // tile,), out_shape=(out, out), in_sp...  54.1 us
    all_to_all x1, blocking collectives, per_device(): lax.all_to_all(ready, OWN, split_axis=0, concat_axis=0, tiled=True)  34.2 us
    all_to_all x3, waiting for transfers between devices, per_device(): lax.all_to_all(ready, OWN, split_axis=0, concat_axis=0, tiled=True)  33.4 us
    ppermute x8, waiting for transfers between devices, send(): return lax.ppermute(x, 'tp', [(i, (i + step) % size) for i in range(size)])  19.8 us
    all_to_all x3, starting transfers between devices, per_device(): lax.all_to_all(ready, OWN, split_axis=0, concat_axis=0, tiled=True)  18.3 us
    ppermute x8, starting transfers between devices, send(): return lax.ppermute(x, 'tp', [(i, (i + step) % size) for i in range(size)])  14.2 us
    all_to_all x1, blocking collectives, per_device(): lax.all_to_all(request.reshape(owners, capacity), OWN, split_axis=0, conc...  13.6 us
    pallas_call x4, Pallas kernels, scatter_rows(): pl.pallas_call(body, out_shape=jax.ShapeDtypeStruct((cells, rows, width),...  11.7 us
  transfers between devices with their start and end apart: 13, of which 8 were waited for; matrix products, arithmetic and copies ran while one was open for 2% of the time, Pallas kernels for 24%

profile of v5, /device:TPU:2, one launch (start us, length us, event | category | flops | bytes accessed | tf_op | source)
XLA Modules:
  0.0 239.0 jit_solution(16754043028368723783)
XLA Ops:
  8.3 13.6 %all_to_all.26 = s32[32,1,2]{2,1,0:T(1,128)S(1)} all-to-all(s32[32,1,2]{2,1,0:T(1,128)S(1)} %bitcast.51), channel_id=1, replica_groups=mesh['section'=4,'seq'=8,'tp'=4] {'section','seq'}, dimensions={0} | all-to-all | bytes 512 | tf_op jit(solution)/shard_map/all_to_all | solution.py:244
  23.8 2.9 %pick_rows.4 = bf16[64,16,1024]{2,1,0:T(8,128)(2,1)} custom-call(s32[24]{0:T(128)} %select_reduce_fusion.position_ref, bf16[24,64,1024]{2,1,0:T(8,128)(2,1)} %bitcast.26), custom_call_target="tpu_custom_call" | custom-call | bytes 1572864 | tf_op jit(solution)/shard_map/pick_rows/pallas_call | solution.py:36
  26.8 5.8 %all-to-all-start.1 = ((bf16[32,2,16,1024]{3,2,1,0:T(8,128)(2,1)}), bf16[32,2,16,1024]{3,2,1,0:T(8,128)(2,1)}, u32[]{:S(2)}, u32[]{:S(2)}) async-start(bf16[32,2,16,1024]{3,2,1,0:T(8,128)(2,1)} %bitcast.33), calls=%async_computation.1 | async-start | bytes 4194304 | tf_op jit(solution)/shard_map/all_to_all | solution.py:279
  32.6 2.9 %pick_rows.5 = bf16[64,16,1024]{2,1,0:T(8,128)(2,1)} custom-call(s32[24]{0:T(128)} %select_reduce_fusion.position_ref, bf16[24,64,1024]{2,1,0:T(8,128)(2,1)} %bitcast.27), custom_call_target="tpu_custom_call" | custom-call | bytes 1572864 | tf_op jit(solution)/shard_map/pick_rows/pallas_call | solution.py:36
  35.6 2.9 %pick_rows.6 = bf16[64,16,1024]{2,1,0:T(8,128)(2,1)} custom-call(s32[24]{0:T(128)} %select_reduce_fusion.position_ref, bf16[24,64,1024]{2,1,0:T(8,128)(2,1)} %bitcast.28), custom_call_target="tpu_custom_call" | custom-call | bytes 1572864 | tf_op jit(solution)/shard_map/pick_rows/pallas_call | solution.py:36
  38.5 3.0 %pick_rows.7 = bf16[64,16,1024]{2,1,0:T(8,128)(2,1)} custom-call(s32[24]{0:T(128)} %select_reduce_fusion.position_ref, bf16[24,64,1024]{2,1,0:T(8,128)(2,1)} %bitcast.29), custom_call_target="tpu_custom_call" | custom-call | bytes 1572864 | tf_op jit(solution)/shard_map/pick_rows/pallas_call | solution.py:36
  41.5 19.1 %all-to-all-done.1 = bf16[32,2,16,1024]{3,2,1,0:T(8,128)(2,1)} async-done(((bf16[32,2,16,1024]{3,2,1,0:T(8,128)(2,1)}), bf16[32,2,16,1024]{3,2,1,0:T(8,128)(2,1)}, u32[]{:S(2)}, u32[]{:S(2)}) %all-to-all-start.1) | async-done | bytes 2097184 | tf_op jit(solution)/shard_map/all_to_all | solution.py:279
  60.6 2.8 %place_rows.4 = bf16[24,16,1024]{2,1,0:T(8,128)(2,1)} custom-call(s32[24]{0:T(128)} %copy-done, bf16[64,16,1024]{2,1,0:T(8,128)(2,1)} %bitcast.10.cells_ref), custom_call_target="tpu_custom_call" | custom-call | bytes 1572864 | tf_op jit(solution)/shard_map/place_rows/pallas_call | solution.py:71
  63.5 34.2 %all_to_all.27 = bf16[32,2,16,1024]{3,2,1,0:T(8,128)(2,1)} all-to-all(bf16[32,2,16,1024]{3,2,1,0:T(8,128)(2,1)} %bitcast.32), channel_id=1, replica_groups=mesh['section'=4,'seq'=8,'tp'=4] {'section','seq'}, dimensions={0} | all-to-all | bytes 4194304 | tf_op jit(solution)/shard_map/all_to_all | solution.py:279
  97.7 2.8 %place_rows.5 = bf16[24,16,1024]{2,1,0:T(8,128)(2,1)} custom-call(s32[24]{0:T(128)} %copy-done, bf16[64,16,1024]{2,1,0:T(8,128)(2,1)} %bitcast.34), custom_call_target="tpu_custom_call" | custom-call | bytes 1572864 | tf_op jit(solution)/shard_map/place_rows/pallas_call | solution.py:71
  100.6 5.8 %all-to-all-start.3 = ((bf16[32,2,16,1024]{3,2,1,0:T(8,128)(2,1)}), bf16[32,2,16,1024]{3,2,1,0:T(8,128)(2,1)}, u32[]{:S(2)}, u32[]{:S(2)}) async-start(bf16[32,2,16,1024]{3,2,1,0:T(8,128)(2,1)} %bitcast.31), calls=%async_computation.3 | async-start | bytes 4194304 | tf_op jit(solution)/shard_map/all_to_all | solution.py:279
  106.4 13.8 %norm_and_project.4 = (bf16[384,1024]{1,0:T(8,128)(2,1)}, bf16[384,1024]{1,0:T(8,128)(2,1)}) custom-call(s32[1]{0:T(128)} %bitcast.here_ref, f32[1,4096]{1,0:T(1,128)} %bitcast.60, bf16[4096,1024]{1,0:T(8,128)(2,1)} %bitcast.52, bf16[4096,1024]{1,0:T(8,128)(2,1)} %bitcast.56, bf16[4,384,1024]{2,1,0:T(8,128)(2,1)} %all-gather.3.cloned.1.call-done.refs_0_), custom_call_target="tpu_custom_call" | custom-call | flops 6442450944 | bytes 19922944 | tf_op jit(solution)/shard_map/norm_and_project/pallas_call | solution.py:149
  120.2 14.2 %all-to-all-done.3 = bf16[32,2,16,1024]{3,2,1,0:T(8,128)(2,1)} async-done(((bf16[32,2,16,1024]{3,2,1,0:T(8,128)(2,1)}), bf16[32,2,16,1024]{3,2,1,0:T(8,128)(2,1)}, u32[]{:S(2)}, u32[]{:S(2)}) %all-to-all-start.3) | async-done | bytes 2097184 | tf_op jit(solution)/shard_map/all_to_all | solution.py:279
  134.4 6.7 %all-to-all-start.4 = ((bf16[32,2,16,1024]{3,2,1,0:T(8,128)(2,1)}), bf16[32,2,16,1024]{3,2,1,0:T(8,128)(2,1)}, u32[]{:S(2)}, u32[]{:S(2)}) async-start(bf16[32,2,16,1024]{3,2,1,0:T(8,128)(2,1)} %bitcast.30), calls=%async_computation.4 | async-start | bytes 4194304 | tf_op jit(solution)/shard_map/all_to_all | solution.py:279
  141.1 2.8 %place_rows.6 = bf16[24,16,1024]{2,1,0:T(8,128)(2,1)} custom-call(s32[24]{0:T(128)} %copy-done, bf16[64,16,1024]{2,1,0:T(8,128)(2,1)} %bitcast.15.cells_ref), custom_call_target="tpu_custom_call" | custom-call | bytes 1572864 | tf_op jit(solution)/shard_map/place_rows/pallas_call | solution.py:71
  143.9 2.0 collective-permute-start
  145.9 2.2 collective-permute-start.1
  148.1 13.5 %norm_and_project.5 = (bf16[384,1024]{1,0:T(8,128)(2,1)}, bf16[384,1024]{1,0:T(8,128)(2,1)}) custom-call(s32[1]{0:T(128)} %bitcast.here_ref, f32[1,4096]{1,0:T(1,128)} %bitcast.61, bf16[4096,1024]{1,0:T(8,128)(2,1)} %bitcast.53, bf16[4096,1024]{1,0:T(8,128)(2,1)} %bitcast.57, bf16[4,384,1024]{2,1,0:T(8,128)(2,1)} %all-gather.5.cloned.1.call-done.refs_0_), custom_call_target="tpu_custom_call" | custom-call | flops 6442450944 | bytes 19922944 | tf_op jit(solution)/shard_map/norm_and_project/pallas_call | solution.py:149
  161.6 4.6 %collective-permute-done.refs_1_ = bf16[384,1024]{1,0:T(8,128)(2,1)} collective-permute-done((bf16[384,1024]{1,0:T(8,128)(2,1)}, bf16[384,1024]{1,0:T(8,128)(2,1)}, u32[]{:S(2)}, u32[]{:S(2)}) %collective-permute-start) | collective-permute-done | bytes 786464 | tf_op jit(solution)/shard_map/ppermute | solution.py:93
  167.2 3.1 %collective-permute-start.3 = (bf16[192,1024]{1,0:T(8,128)(2,1)S(1)}, bf16[192,1024]{1,0:T(8,128)(2,1)}, u32[]{:S(2)}, u32[]{:S(2)}) collective-permute-start(bf16[192,1024]{1,0:T(8,128)(2,1)S(1)} %slice.13), channel_id=1, source_target_pairs={{0,3},{1,0},{2,1},{3,2},{4,7},{5,4},{6,5},{7,6},{8,11},{9,8},{10,9... | collective-permute-start | bytes 1179656 | tf_op jit(solution)/shard_map/ppermute | solution.py:93
  170.3 1.8 slice.12
  172.1 2.8 %place_rows.7 = bf16[24,16,1024]{2,1,0:T(8,128)(2,1)} custom-call(s32[24]{0:T(128)} %copy-done, bf16[64,16,1024]{2,1,0:T(8,128)(2,1)} %bitcast.18.cells_ref), custom_call_target="tpu_custom_call" | custom-call | bytes 1572864 | tf_op jit(solution)/shard_map/place_rows/pallas_call | solution.py:71
  175.2 3.1 %collective-permute-start.5 = (bf16[384,1024]{1,0:T(8,128)(2,1)}, bf16[384,1024]{1,0:T(8,128)(2,1)}, u32[]{:S(2)}, u32[]{:S(2)}) collective-permute-start(bf16[384,1024]{1,0:T(8,128)(2,1)} %bitcast.41), channel_id=1, source_target_pairs={{0,3},{1,0},{2,1},{3,2},{4,7},{5,4},{6,5},{7,6},{8,11},{9,8},{10,9... | collective-permute-start | bytes 2359304 | tf_op jit(solution)/shard_map/ppermute | solution.py:93
  179.0 6.7 %collective-permute-done.2.refs_3_ = bf16[192,1024]{1,0:T(8,128)(2,1)} collective-permute-done((bf16[192,1024]{1,0:T(8,128)(2,1)}, bf16[192,1024]{1,0:T(8,128)(2,1)}, u32[]{:S(2)}, u32[]{:S(2)}) %collective-permute-start.2) | collective-permute-done | bytes 393248 | tf_op jit(solution)/shard_map/ppermute | solution.py:93
  185.7 13.4 %norm_and_project.6 = (bf16[384,1024]{1,0:T(8,128)(2,1)}, bf16[384,1024]{1,0:T(8,128)(2,1)}) custom-call(s32[1]{0:T(128)} %bitcast.here_ref, f32[1,4096]{1,0:T(1,128)} %bitcast.62, bf16[4096,1024]{1,0:T(8,128)(2,1)} %bitcast.54, bf16[4096,1024]{1,0:T(8,128)(2,1)} %bitcast.58, bf16[384,1024]{1,0:T(8,128)(2,1)} %bitcast.39, ...), custom_call_target="tpu_custom_call" | custom-call | flops 6442450944 | bytes 19922944 | tf_op jit(solution)/shard_map/norm_and_project/pallas_call | solution.py:149
  199.1 1.4 collective-permute-done.4.refs_1_
  200.5 1.0 slice.14
  201.6 1.0 slice.15
  202.7 3.5 %collective-permute-start.7 = (bf16[192,1024]{1,0:T(8,128)(2,1)S(1)}, bf16[192,1024]{1,0:T(8,128)(2,1)}, u32[]{:S(2)}, u32[]{:S(2)}) collective-permute-start(bf16[192,1024]{1,0:T(8,128)(2,1)S(1)} %slice.15), channel_id=1, source_target_pairs={{0,3},{1,0},{2,1},{3,2},{4,7},{5,4},{6,5},{7,6},{8,11},{9,8},{10,9... | collective-permute-start | bytes 1179656 | tf_op jit(solution)/shard_map/ppermute | solution.py:93
  206.1 5.8 %collective-permute-done.6.refs_3_ = bf16[192,1024]{1,0:T(8,128)(2,1)S(1)} collective-permute-done((bf16[192,1024]{1,0:T(8,128)(2,1)S(1)}, bf16[192,1024]{1,0:T(8,128)(2,1)S(1)}, u32[]{:S(2)}, u32[]{:S(2)}) %collective-permute-start.6) | collective-permute-done | bytes 393248 | tf_op jit(solution)/shard_map/ppermute | solution.py:93
  212.7 13.4 %norm_and_project.7 = (bf16[384,1024]{1,0:T(8,128)(2,1)}, bf16[384,1024]{1,0:T(8,128)(2,1)}) custom-call(s32[1]{0:T(128)} %bitcast.here_ref, f32[1,4096]{1,0:T(1,128)} %bitcast.63, bf16[4096,1024]{1,0:T(8,128)(2,1)} %bitcast.55, bf16[4096,1024]{1,0:T(8,128)(2,1)} %bitcast.59, bf16[384,1024]{1,0:T(8,128)(2,1)} %bitcast.42, ...), custom_call_target="tpu_custom_call" | custom-call | flops 6442450944 | bytes 19922944 | tf_op jit(solution)/shard_map/norm_and_project/pallas_call | solution.py:149
  226.1 6.0 %attention.1 = bf16[384,1024]{1,0:T(8,128)(2,1)} custom-call(s32[6]{0:T(128)} %count_ref.1, bf16[384,1024]{1,0:T(8,128)(2,1)} %query_ref.1, bf16[6,64,1024]{2,1,0:T(8,128)(2,1)} %bitcast.43, bf16[6,64,1024]{2,1,0:T(8,128)(2,1)} %bitcast.45, bf16[6,64,1024]{2,1,0:T(8,128)(2,1)} %bitcast.47, bf16[6,64,1024]{2,1,0:T(8,128)(2,1)} %bitcast.49, ...), custom_call_target="tpu_custom_call" | custom-call | flops 402653184 | bytes 7864320 | tf_op jit(solution)/shard_map/attention/pallas_call | solution.py:213
  (29 shorter events, 6.7 us)
Async XLA Ops:
  8.1 18.6 %copy-start = (s32[24]{0:T(128)}, s32[24]{0:T(128)S(1)}, u32[]{:S(2)}) copy-start(s32[24]{0:T(128)S(1)} %multiply_add_fusion.position_ref) | copy-start | bytes 292
  26.8 33.8 %all-to-all-start.1 = ((bf16[32,2,16,1024]{3,2,1,0:T(8,128)(2,1)}), bf16[32,2,16,1024]{3,2,1,0:T(8,128)(2,1)}, u32[]{:S(2)}, u32[]{:S(2)}) async-start(bf16[32,2,16,1024]{3,2,1,0:T(8,128)(2,1)} %bitcast.33), calls=%async_computation.1 | async-start | bytes 4194304 | tf_op jit(solution)/shard_map/all_to_all | solution.py:279
  32.6 73.8 %all-gather.3.cloned.1.call-start = ((), (), s32[]{:S(2)}) async-start(), calls=%async_computation.5 | async-start | bytes 3932160 | tf_op jit(solution)/shard_map/all_gather | solution.py:286
  63.4 84.7 %all-gather.5.cloned.1.call-start = ((), (), s32[]{:S(2)}) async-start(), calls=%async_computation.6 | async-start | bytes 3932160 | tf_op jit(solution)/shard_map/all_gather | solution.py:286
  100.6 33.8 %all-to-all-start.3 = ((bf16[32,2,16,1024]{3,2,1,0:T(8,128)(2,1)}), bf16[32,2,16,1024]{3,2,1,0:T(8,128)(2,1)}, u32[]{:S(2)}, u32[]{:S(2)}) async-start(bf16[32,2,16,1024]{3,2,1,0:T(8,128)(2,1)} %bitcast.31), calls=%async_computation.3 | async-start | bytes 4194304 | tf_op jit(solution)/shard_map/all_to_all | solution.py:279
  134.4 37.7 %all-to-all-start.4 = ((bf16[32,2,16,1024]{3,2,1,0:T(8,128)(2,1)}), bf16[32,2,16,1024]{3,2,1,0:T(8,128)(2,1)}, u32[]{:S(2)}, u32[]{:S(2)}) async-start(bf16[32,2,16,1024]{3,2,1,0:T(8,128)(2,1)} %bitcast.30), calls=%async_computation.4 | async-start | bytes 4194304 | tf_op jit(solution)/shard_map/all_to_all | solution.py:279
  143.9 22.3 %collective-permute-start = (bf16[384,1024]{1,0:T(8,128)(2,1)}, bf16[384,1024]{1,0:T(8,128)(2,1)}, u32[]{:S(2)}, u32[]{:S(2)}) collective-permute-start(bf16[384,1024]{1,0:T(8,128)(2,1)} %bitcast.37), channel_id=1, source_target_pairs={{0,1},{1,2},{2,3},{3,0},{4,5},{5,6},{6,7},{7,4},{8,9},{9,10},{10,1... | collective-permute-start | bytes 2359304 | tf_op jit(solution)/shard_map/ppermute | solution.py:93
  145.9 20.3 %collective-permute-start.1 = (bf16[384,1024]{1,0:T(8,128)(2,1)}, bf16[384,1024]{1,0:T(8,128)(2,1)}, u32[]{:S(2)}, u32[]{:S(2)}) collective-permute-start(bf16[384,1024]{1,0:T(8,128)(2,1)} %bitcast.38), channel_id=1, source_target_pairs={{0,3},{1,0},{2,1},{3,2},{4,7},{5,4},{6,5},{7,6},{8,11},{9,8},{10,9... | collective-permute-start | bytes 2359304 | tf_op jit(solution)/shard_map/ppermute | solution.py:93
  167.2 11.8 %collective-permute-start.3 = (bf16[192,1024]{1,0:T(8,128)(2,1)S(1)}, bf16[192,1024]{1,0:T(8,128)(2,1)}, u32[]{:S(2)}, u32[]{:S(2)}) collective-permute-start(bf16[192,1024]{1,0:T(8,128)(2,1)S(1)} %slice.13), channel_id=1, source_target_pairs={{0,3},{1,0},{2,1},{3,2},{4,7},{5,4},{6,5},{7,6},{8,11},{9,8},{10,9... | collective-permute-start | bytes 1179656 | tf_op jit(solution)/shard_map/ppermute | solution.py:93
  172.1 13.6 %collective-permute-start.2 = (bf16[192,1024]{1,0:T(8,128)(2,1)}, bf16[192,1024]{1,0:T(8,128)(2,1)}, u32[]{:S(2)}, u32[]{:S(2)}) collective-permute-start(bf16[192,1024]{1,0:T(8,128)(2,1)} %slice.12), channel_id=1, source_target_pairs={{0,1},{1,2},{2,3},{3,0},{4,5},{5,6},{6,7},{7,4},{8,9},{9,10},{10,1... | collective-permute-start | bytes 1179656 | tf_op jit(solution)/shard_map/ppermute | solution.py:93
  174.9 25.6 %collective-permute-start.4 = (bf16[384,1024]{1,0:T(8,128)(2,1)}, bf16[384,1024]{1,0:T(8,128)(2,1)}, u32[]{:S(2)}, u32[]{:S(2)}) collective-permute-start(bf16[384,1024]{1,0:T(8,128)(2,1)} %bitcast.40), channel_id=1, source_target_pairs={{0,1},{1,2},{2,3},{3,0},{4,5},{5,6},{6,7},{7,4},{8,9},{9,10},{10,1... | collective-permute-start | bytes 2359304 | tf_op jit(solution)/shard_map/ppermute | solution.py:93
  175.2 25.3 %collective-permute-start.5 = (bf16[384,1024]{1,0:T(8,128)(2,1)}, bf16[384,1024]{1,0:T(8,128)(2,1)}, u32[]{:S(2)}, u32[]{:S(2)}) collective-permute-start(bf16[384,1024]{1,0:T(8,128)(2,1)} %bitcast.41), channel_id=1, source_target_pairs={{0,3},{1,0},{2,1},{3,2},{4,7},{5,4},{6,5},{7,6},{8,11},{9,8},{10,9... | collective-permute-start | bytes 2359304 | tf_op jit(solution)/shard_map/ppermute | solution.py:93
  201.6 10.4 %collective-permute-start.6 = (bf16[192,1024]{1,0:T(8,128)(2,1)S(1)}, bf16[192,1024]{1,0:T(8,128)(2,1)S(1)}, u32[]{:S(2)}, u32[]{:S(2)}) collective-permute-start(bf16[192,1024]{1,0:T(8,128)(2,1)S(1)} %slice.14), channel_id=1, source_target_pairs={{0,1},{1,2},{2,3},{3,0},{4,5},{5,6},{6,7},{7,4},{8,9},{9,10},{10,1... | collective-permute-start | bytes 1179656 | tf_op jit(solution)/shard_map/ppermute | solution.py:93
  202.7 9.8 %collective-permute-start.7 = (bf16[192,1024]{1,0:T(8,128)(2,1)S(1)}, bf16[192,1024]{1,0:T(8,128)(2,1)}, u32[]{:S(2)}, u32[]{:S(2)}) collective-permute-start(bf16[192,1024]{1,0:T(8,128)(2,1)S(1)} %slice.15), channel_id=1, source_target_pairs={{0,3},{1,0},{2,1},{3,2},{4,7},{5,4},{6,5},{7,6},{8,11},{9,8},{10,9... | collective-permute-start | bytes 1179656 | tf_op jit(solution)/shard_map/ppermute | solution.py:93
  212.0 0.7 copy-start.1
Sparse Core Ops, SparseCore 0:
  63.6 39.5 all-gather.2
  104.8 39.7 all-gather.4
